TPU v7x, 32 devices: a whole 2x2x4 slice. The times are simulated.
32 devices in a mesh: dp: 4 (over y, core), blk: 8 (over z, x).
Axes of the slice: x: 2, y: 2, z: 4, core: 2. Of those that a mesh axis runs over, the one named last changes fastest.
Arguments:
- inputs: bfloat16 [4, 4, 1024, 768], P(None, 'dp', 'blk'), may hold values from -6 to 6
- segment_ids: int32 [4, 4, 1024], P(None, 'dp', 'blk'), may hold values from 0 to 1023, as said below
- query_weight: bfloat16 [768, 768], P('dp', 'blk'), may hold values from -0.21875 to 0.21875
- query_bias: bfloat16 [768], P('blk'), may hold values from -3 to 3
- key_weight: bfloat16 [768, 768], P('dp', 'blk'), may hold values from -0.21875 to 0.21875
- value_weight: bfloat16 [768, 768], P('dp', 'blk'), may hold values from -0.21875 to 0.21875
- value_bias: bfloat16 [768], P('blk'), may hold values from -3 to 3
- output_weight: bfloat16 [768, 768], P('dp', 'blk'), may hold values from -1.25 to 1.25
- output_bias: bfloat16 [768], P('blk'), may hold values from -3 to 3
- first_gain: bfloat16 [768], P('blk'), may hold values from 0.5 to 1.5
- first_shift: bfloat16 [768], P('blk'), may hold values from -3 to 3
- up_weight: bfloat16 [768, 3072], P('dp', 'blk'), may hold values from -0.21875 to 0.21875
- up_bias: bfloat16 [3072], P('blk'), may hold values from -3 to 3
- down_weight: bfloat16 [3072, 768], P('dp', 'blk'), may hold values from -0.109375 to 0.109375
- down_bias: bfloat16 [768], P('blk'), may hold values from -3 to 3
- second_gain: bfloat16 [768], P('blk'), may hold values from 0.5 to 1.5
- second_shift: bfloat16 [768], P('blk'), may hold values from -3 to 3
- cotangent: bfloat16 [4, 4, 1024, 768], P(None, 'dp', 'blk'), may hold values from -6 to 6
Outputs:
- layer_output: bfloat16 [4, 4, 1024, 768], P(None, 'dp', 'blk')
- input_grad: bfloat16 [4, 4, 1024, 768], P(None, 'dp', 'blk')
- grad_query_weight: float32 [768, 768], P('dp', 'blk')
- grad_query_bias: float32 [768], P('blk')
- grad_key_weight: float32 [768, 768], P('dp', 'blk')
- grad_value_weight: float32 [768, 768], P('dp', 'blk')
- grad_value_bias: float32 [768], P('blk')
- grad_output_weight: float32 [768, 768], P('dp', 'blk')
- grad_output_bias: float32 [768], P('blk')
- grad_first_gain: float32 [768], P('blk')
- grad_first_shift: float32 [768], P('blk')
- grad_up_weight: float32 [768, 3072], P('dp', 'blk')
- grad_up_bias: float32 [3072], P('blk')
- grad_down_weight: float32 [3072, 768], P('dp', 'blk')
- grad_down_bias: float32 [768], P('blk')
- grad_second_gain: float32 [768], P('blk')
- grad_second_shift: float32 [768], P('blk')
Inputs may be any that keep to these rules, and one draw needn't show every extreme that they name: `segment_ids`: along each row the ids never fall, and a passage is a run of equal ids. The last passage of every row has id 1024 - 1, and every other passage has a smaller id. Among the rows of one index of dp (all micro-batches), one row holds a passage that begins among the first 128 positions and ends among the last 128.
All inputs are finite; a program needn't handle non-finite values.
Results may differ from a plain program's by a relative error of at most 0.019.
Values may be sent and summed in bfloat16 or wider, within the bound.
A program may use at most 256 MiB of HBM per device.

v0:
```python
from functools import partial

import jax
import jax.numpy as jnp
from jax import lax
from jax.sharding import PartitionSpec as P

HEADS = 12
HD = 64


EPSILON = 1e-12
NEGATIVE = -1e30


def product(left, right, form):
    return jnp.einsum(form, left, right, preferred_element_type=jnp.float32)


def normalize(hidden, gain, shift):
    centred = hidden - jnp.mean(hidden, axis=-1, keepdims=True)
    scale_inv = lax.rsqrt(jnp.mean(centred * centred, axis=-1, keepdims=True) + EPSILON)
    normed = centred * scale_inv
    return (normed * gain + shift, normed, scale_inv)


def normalize_back(grad_normed, normed, scale_inv):
    centred_grad = grad_normed - jnp.mean(grad_normed, axis=-1, keepdims=True)
    return scale_inv * (
        centred_grad - normed * jnp.mean(grad_normed * normed, axis=-1, keepdims=True)
    )


def same_passage(query_pair, key_pair):
    return jnp.all(query_pair[:, :, None, :] == key_pair[:, None, :, :], axis=-1)[:, None]


def micro_step(shared, tokens, passage_ids, cotan):
    (
        weight_query,
        weight_key,
        weight_value,
        weight_out,
        weight_up,
        weight_down,
        bias_query,
        bias_value,
        bias_out,
        gain_first,
        shift_first,
        bias_up,
        bias_down,
        gain_second,
        shift_second,
    ) = shared
    bias_query = bias_query.astype(jnp.float32)
    bias_value = bias_value.astype(jnp.float32)
    bias_out = bias_out.astype(jnp.float32)
    gain_first = gain_first.astype(jnp.float32)
    shift_first = shift_first.astype(jnp.float32)
    bias_up = bias_up.astype(jnp.float32)
    bias_down = bias_down.astype(jnp.float32)
    gain_second = gain_second.astype(jnp.float32)
    shift_second = shift_second.astype(jnp.float32)
    row_count, seq_count, width = tokens.shape
    token_count = row_count * seq_count
    scale = HD ** (-0.5)
    flat = tokens.reshape(token_count, width)
    queries = (product(flat, weight_query, "md,de->me") + bias_query).astype(jnp.bfloat16)
    keys = product(flat, weight_key, "md,de->me").astype(jnp.bfloat16)
    values = (product(flat, weight_value, "md,de->me") + bias_value).astype(jnp.bfloat16)
    query_four = queries.reshape(row_count, seq_count, HEADS, HD)
    pair_local = jnp.stack((passage_ids // 256, passage_ids % 256), axis=-1).astype(jnp.bfloat16)
    key_rows = keys.reshape(row_count, seq_count, width)
    value_rows = values.reshape(row_count, seq_count, width)
    key_local = key_rows.reshape(row_count, seq_count, HEADS, HD)
    value_local = value_rows.reshape(row_count, seq_count, HEADS, HD)
    running_max = jnp.full((row_count, HEADS, seq_count), NEGATIVE, jnp.float32)
    running_acc = jnp.zeros((row_count, seq_count, HEADS, HD), jnp.float32)
    key_piece = lax.all_gather(key_rows, "blk", axis=1, tiled=True)
    value_piece = lax.all_gather(value_rows, "blk", axis=1, tiled=True)
    pair_piece = lax.all_gather(pair_local, "blk", axis=1, tiled=True)
    count = key_piece.shape[1]
    key_four = key_piece.reshape(row_count, count, HEADS, HD)
    value_four = value_piece.reshape(row_count, count, HEADS, HD)
    allowed = same_passage(pair_local, pair_piece)
    scores = jnp.where(allowed, product(query_four, key_four, "rqhd,rkhd->rhqk") * scale, NEGATIVE)
    fresh_max = jnp.maximum(running_max, jnp.max(scores, axis=-1))
    weights = jnp.where(allowed, jnp.exp(scores - fresh_max[..., None]), 0.0)
    decay = jnp.exp(running_max - fresh_max)
    running_sum = jnp.sum(weights, axis=-1)
    mixed = product(weights.astype(jnp.bfloat16), value_four, "rhqk,rkhd->rqhd")
    running_acc = running_acc * jnp.swapaxes(decay, 1, 2)[..., None] + mixed
    running_max, running_sum, running_acc = (fresh_max, running_sum, running_acc)
    log_total = running_max + jnp.log(running_sum)
    attended = running_acc / jnp.swapaxes(running_sum, 1, 2)[..., None]
    context = attended.reshape(token_count, width).astype(jnp.bfloat16)
    branch = product(context, weight_out, "md,de->me") + bias_out
    first, normed_first, inv_first = normalize(
        flat.astype(jnp.float32) + branch, gain_first, shift_first
    )
    first_low = first.astype(jnp.bfloat16)
    inner = product(first_low, weight_up, "md,df->mf") + bias_up
    activation, gelu_pull = jax.vjp(partial(jax.nn.gelu, approximate=False), inner)
    hidden = activation.astype(jnp.bfloat16)
    second = product(hidden, weight_down, "mf,fd->md") + bias_down
    output, normed_second, inv_second = normalize(first + second, gain_second, shift_second)
    upstream = cotan.reshape(token_count, width).astype(jnp.float32)
    grad_gain_second = jnp.sum(upstream * normed_second, axis=0, keepdims=True)
    grad_shift_second = jnp.sum(upstream, axis=0, keepdims=True)
    grad_sum_second = normalize_back(upstream * gain_second, normed_second, inv_second)
    grad_second = grad_sum_second.astype(jnp.bfloat16)
    grad_weight_down = product(hidden, grad_second, "mf,md->fd")
    grad_bias_down = jnp.sum(grad_second.astype(jnp.float32), axis=0, keepdims=True)
    grad_inner = gelu_pull(product(grad_second, weight_down, "md,fd->mf"))[0].astype(jnp.bfloat16)
    grad_weight_up = product(first_low, grad_inner, "md,mf->df")
    grad_bias_up = jnp.sum(grad_inner.astype(jnp.float32), axis=0, keepdims=True)
    grad_first = grad_sum_second + product(grad_inner, weight_up, "mf,df->md")
    grad_gain_first = jnp.sum(grad_first * normed_first, axis=0, keepdims=True)
    grad_shift_first = jnp.sum(grad_first, axis=0, keepdims=True)
    grad_sum_first = normalize_back(grad_first * gain_first, normed_first, inv_first)
    grad_branch = grad_sum_first.astype(jnp.bfloat16)
    grad_weight_out = product(context, grad_branch, "md,me->de")
    grad_bias_out = jnp.sum(grad_branch.astype(jnp.float32), axis=0, keepdims=True)
    grad_context = product(grad_branch, weight_out, "me,de->md").astype(jnp.bfloat16)
    grad_context_four = grad_context.reshape(row_count, seq_count, HEADS, HD)
    delta = jnp.swapaxes(jnp.sum(grad_context_four.astype(jnp.float32) * attended, axis=-1), 1, 2)
    key_piece = lax.all_gather(key_rows, "blk", axis=1, tiled=True)
    value_piece = lax.all_gather(value_rows, "blk", axis=1, tiled=True)
    pair_piece = lax.all_gather(pair_local, "blk", axis=1, tiled=True)
    count = key_piece.shape[1]
    key_four = key_piece.reshape(row_count, count, HEADS, HD)
    value_four = value_piece.reshape(row_count, count, HEADS, HD)
    allowed = same_passage(pair_local, pair_piece)
    scores = jnp.where(allowed, product(query_four, key_four, "rqhd,rkhd->rhqk") * scale, NEGATIVE)
    probs = jnp.where(allowed, jnp.exp(scores - log_total[..., None]), 0.0)
    grad_probs = product(grad_context_four, value_four, "rqhd,rkhd->rhqk")
    grad_scores = (probs * (grad_probs - delta[..., None])).astype(jnp.bfloat16)
    grad_query_acc = product(grad_scores, key_four, "rhqk,rkhd->rqhd") * scale
    grad_queries = grad_query_acc.reshape(token_count, width).astype(jnp.bfloat16)
    pair_wide = pair_local.astype(jnp.float32)
    sent = (
        queries.reshape(row_count, seq_count, width).astype(jnp.float32),
        grad_context.reshape(row_count, seq_count, width).astype(jnp.float32),
        jnp.swapaxes(log_total, 1, 2),
        jnp.swapaxes(delta, 1, 2),
        pair_wide,
    )
    query_piece = lax.all_gather(sent[0], "blk", axis=1, tiled=True)
    context_piece = lax.all_gather(sent[1], "blk", axis=1, tiled=True)
    total_piece = lax.all_gather(sent[2], "blk", axis=1, tiled=True)
    delta_piece = lax.all_gather(sent[3], "blk", axis=1, tiled=True)
    pair_piece = lax.all_gather(sent[4], "blk", axis=1, tiled=True)
    count = query_piece.shape[1]
    query_part = query_piece.astype(jnp.bfloat16).reshape(row_count, count, HEADS, HD)
    context_part = context_piece.astype(jnp.bfloat16).reshape(row_count, count, HEADS, HD)
    total_part = jnp.swapaxes(total_piece, 1, 2)
    delta_part = jnp.swapaxes(delta_piece, 1, 2)
    allowed = same_passage(pair_piece, pair_wide)
    scores = jnp.where(allowed, product(query_part, key_local, "rqhd,rkhd->rhqk") * scale, NEGATIVE)
    probs = jnp.where(allowed, jnp.exp(scores - total_part[..., None]), 0.0)
    grad_value_acc = product(probs.astype(jnp.bfloat16), context_part, "rhqk,rqhd->rkhd")
    grad_probs = product(context_part, value_local, "rqhd,rkhd->rhqk")
    grad_scores = (probs * (grad_probs - delta_part[..., None])).astype(jnp.bfloat16)
    grad_key_acc = product(grad_scores, query_part, "rhqk,rqhd->rkhd") * scale
    grad_key_acc, grad_value_acc = (grad_key_acc, grad_value_acc)
    grad_keys = grad_key_acc.reshape(token_count, width).astype(jnp.bfloat16)
    grad_values = grad_value_acc.reshape(token_count, width).astype(jnp.bfloat16)
    grad_weight_query = product(flat, grad_queries, "md,me->de")
    grad_bias_query = jnp.sum(grad_queries.astype(jnp.float32), axis=0, keepdims=True)
    grad_weight_key = product(flat, grad_keys, "md,me->de")
    grad_weight_value = product(flat, grad_values, "md,me->de")
    grad_bias_value = jnp.sum(grad_values.astype(jnp.float32), axis=0, keepdims=True)
    grad_tokens = (
        grad_sum_first
        + product(grad_queries, weight_query, "me,de->md")
        + product(grad_keys, weight_key, "me,de->md")
        + product(grad_values, weight_value, "me,de->md")
    )
    contributions = (
        grad_weight_query,
        grad_weight_key,
        grad_weight_value,
        grad_weight_out,
        grad_weight_up,
        grad_weight_down,
        grad_bias_query,
        grad_bias_value,
        grad_bias_out,
        grad_gain_first,
        grad_shift_first,
        grad_bias_up,
        grad_bias_down,
        grad_gain_second,
        grad_shift_second,
    )
    return (
        output.astype(jnp.bfloat16).reshape(row_count, seq_count, width),
        grad_tokens.astype(jnp.bfloat16).reshape(row_count, seq_count, width),
        contributions,
    )


def on_device(
    inputs,
    segment_ids,
    query_weight,
    query_bias,
    key_weight,
    value_weight,
    value_bias,
    output_weight,
    output_bias,
    first_gain,
    first_shift,
    up_weight,
    up_bias,
    down_weight,
    down_bias,
    second_gain,
    second_shift,
    cotangent,
):
    outputs = []
    input_grads = []
    totals = None
    for batch_index in range(inputs.shape[0]):
        widened = (
            lax.all_gather(query_weight, "blk", axis=1, tiled=True),
            lax.all_gather(key_weight, "blk", axis=1, tiled=True),
            lax.all_gather(value_weight, "blk", axis=1, tiled=True),
            lax.all_gather(output_weight, "blk", axis=1, tiled=True),
            lax.all_gather(up_weight, "blk", axis=1, tiled=True),
            lax.all_gather(down_weight, "blk", axis=1, tiled=True),
            lax.all_gather(query_bias.reshape(1, -1), "blk", axis=1, tiled=True),
            lax.all_gather(value_bias.reshape(1, -1), "blk", axis=1, tiled=True),
            lax.all_gather(output_bias.reshape(1, -1), "blk", axis=1, tiled=True),
            lax.all_gather(first_gain.reshape(1, -1), "blk", axis=1, tiled=True),
            lax.all_gather(first_shift.reshape(1, -1), "blk", axis=1, tiled=True),
            lax.all_gather(up_bias.reshape(1, -1), "blk", axis=1, tiled=True),
            lax.all_gather(down_bias.reshape(1, -1), "blk", axis=1, tiled=True),
            lax.all_gather(second_gain.reshape(1, -1), "blk", axis=1, tiled=True),
            lax.all_gather(second_shift.reshape(1, -1), "blk", axis=1, tiled=True),
        )
        complete = (
            lax.all_gather(widened[0], "dp", axis=0, tiled=True),
            lax.all_gather(widened[1], "dp", axis=0, tiled=True),
            lax.all_gather(widened[2], "dp", axis=0, tiled=True),
            lax.all_gather(widened[3], "dp", axis=0, tiled=True),
            lax.all_gather(widened[4], "dp", axis=0, tiled=True),
            lax.all_gather(widened[5], "dp", axis=0, tiled=True),
        )
        shared = tuple(complete) + tuple(widened[6:])
        layer_out, layer_grad, contributions = micro_step(
            shared, inputs[batch_index], segment_ids[batch_index], cotangent[batch_index]
        )
        outputs.append(layer_out)
        input_grads.append(layer_grad)
        if totals is None:
            totals = contributions
        else:
            totals = tuple((earlier + latest for earlier, latest in zip(totals, contributions)))
    narrowed = (
        lax.psum_scatter(totals[0], "blk", scatter_dimension=1, tiled=True),
        lax.psum_scatter(totals[1], "blk", scatter_dimension=1, tiled=True),
        lax.psum_scatter(totals[2], "blk", scatter_dimension=1, tiled=True),
        lax.psum_scatter(totals[3], "blk", scatter_dimension=1, tiled=True),
        lax.psum_scatter(totals[4], "blk", scatter_dimension=1, tiled=True),
        lax.psum_scatter(totals[5], "blk", scatter_dimension=1, tiled=True),
        lax.psum_scatter(totals[6], "blk", scatter_dimension=1, tiled=True),
        lax.psum_scatter(totals[7], "blk", scatter_dimension=1, tiled=True),
        lax.psum_scatter(totals[8], "blk", scatter_dimension=1, tiled=True),
        lax.psum_scatter(totals[9], "blk", scatter_dimension=1, tiled=True),
        lax.psum_scatter(totals[10], "blk", scatter_dimension=1, tiled=True),
        lax.psum_scatter(totals[11], "blk", scatter_dimension=1, tiled=True),
        lax.psum_scatter(totals[12], "blk", scatter_dimension=1, tiled=True),
        lax.psum_scatter(totals[13], "blk", scatter_dimension=1, tiled=True),
        lax.psum_scatter(totals[14], "blk", scatter_dimension=1, tiled=True),
    )
    matrix_sums = (
        lax.psum_scatter(narrowed[0], "dp", scatter_dimension=0, tiled=True),
        lax.psum_scatter(narrowed[1], "dp", scatter_dimension=0, tiled=True),
        lax.psum_scatter(narrowed[2], "dp", scatter_dimension=0, tiled=True),
        lax.psum_scatter(narrowed[3], "dp", scatter_dimension=0, tiled=True),
        lax.psum_scatter(narrowed[4], "dp", scatter_dimension=0, tiled=True),
        lax.psum_scatter(narrowed[5], "dp", scatter_dimension=0, tiled=True),
    )
    vector_sums = lax.psum(
        (
            narrowed[6],
            narrowed[7],
            narrowed[8],
            narrowed[9],
            narrowed[10],
            narrowed[11],
            narrowed[12],
            narrowed[13],
            narrowed[14],
        ),
        "dp",
    )
    return (
        jnp.stack(outputs),
        jnp.stack(input_grads),
        matrix_sums[0],
        vector_sums[0].reshape(-1),
        matrix_sums[1],
        matrix_sums[2],
        vector_sums[1].reshape(-1),
        matrix_sums[3],
        vector_sums[2].reshape(-1),
        vector_sums[3].reshape(-1),
        vector_sums[4].reshape(-1),
        matrix_sums[4],
        vector_sums[5].reshape(-1),
        matrix_sums[5],
        vector_sums[6].reshape(-1),
        vector_sums[7].reshape(-1),
        vector_sums[8].reshape(-1),
    )


def solution(mesh):
    in_specs = (
        P(None, "dp", "blk", None),
        P(None, "dp", "blk"),
        P("dp", "blk"),
        P("blk"),
        P("dp", "blk"),
        P("dp", "blk"),
        P("blk"),
        P("dp", "blk"),
        P("blk"),
        P("blk"),
        P("blk"),
        P("dp", "blk"),
        P("blk"),
        P("dp", "blk"),
        P("blk"),
        P("blk"),
        P("blk"),
        P(None, "dp", "blk", None),
    )
    out_specs = (
        P(None, "dp", "blk", None),
        P(None, "dp", "blk", None),
        P("dp", "blk"),
        P("blk"),
        P("dp", "blk"),
        P("dp", "blk"),
        P("blk"),
        P("dp", "blk"),
        P("blk"),
        P("blk"),
        P("blk"),
        P("dp", "blk"),
        P("blk"),
        P("dp", "blk"),
        P("blk"),
        P("blk"),
        P("blk"),
    )
    return jax.shard_map(
        on_device, mesh=mesh, in_specs=in_specs, out_specs=out_specs, check_vma=False
    )
```

profile of v0, /device:TPU:1, one launch (start us, length us, event | category | flops | bytes accessed | tf_op | source)
XLA Modules:
  0.0 2414.5 jit_solution(14767455204489581498)
XLA Ops:
  8.1 26.3 %all_gather.110 = bf16[192,768]{0,1:T(8,128)(2,1)S(1)} all-gather(bf16[192,96]{0,1:T(8,128)(2,1)S(1)} %copy.274), channel_id=1, replica_groups=mesh['dp'=4,'blk'=8] {'blk'}, dimensions={1}, use_global_device_ids=true | all-gather | bytes 331776 | tf_op jit(solution)/shard_map/all_gather | solution.py:230
  36.3 24.9 %all_gather.113 = bf16[192,768]{0,1:T(8,128)(2,1)S(1)} all-gather(bf16[192,96]{0,1:T(8,128)(2,1)S(1)} %copy.277), channel_id=1, replica_groups=mesh['dp'=4,'blk'=8] {'blk'}, dimensions={1}, use_global_device_ids=true | all-gather | bytes 331776 | tf_op jit(solution)/shard_map/all_gather | solution.py:231
  63.8 24.9 %all_gather.107 = bf16[192,768]{0,1:T(8,128)(2,1)S(1)} all-gather(bf16[192,96]{0,1:T(8,128)(2,1)S(1)} %copy.271), channel_id=1, replica_groups=mesh['dp'=4,'blk'=8] {'blk'}, dimensions={1}, use_global_device_ids=true | all-gather | bytes 331776 | tf_op jit(solution)/shard_map/all_gather | solution.py:229
  95.2 29.9 %all-reduce.9 = (bf16[768]{0:T(1024)(128)(2,1)S(1)}, bf16[768]{0:T(1024)(128)(2,1)}, bf16[768]{0:T(1024)(128)(2,1)S(1)}, bf16[768]{0:T(1024)(128)(2,1)}, bf16[76...) all-reduce(bf16[768]{0:T(1024)(128)(2,1)S(1)} %dynamic-update-slice, ...), channel_id=4, replica_groups=mesh['dp'=4,'blk'=8] {'blk'}, use_global_device_ids=true, to_apply=%add.1 | all-reduce | flops 6144 | bytes 24576
  128.3 25.1 %all_gather.117 = bf16[192,768]{0,1:T(8,128)(2,1)S(1)} all-gather(bf16[192,96]{0,1:T(8,128)(2,1)} %copy.280), channel_id=1, replica_groups=mesh['dp'=4,'blk'=8] {'blk'}, dimensions={1}, use_global_device_ids=true | all-gather | bytes 331776 | tf_op jit(solution)/shard_map/all_gather | solution.py:232
  161.5 17.7 all-gather.67.cloned.1.call-done
  179.3 19.1 all-gather.55.cloned.1.call-done
  203.7 21.8 all-gather.29
  228.0 15.9 all_gather.264
  244.4 12.7 all_gather.258
  257.6 14.6 all_gather.106
  272.8 12.8 all_gather.261
  310.8 42.8 %all-gather.75.cloned.1.call-done = bf16[1024,768]{1,0:T(8,128)(2,1)} async-done(((bf16[128,768]{1,0:T(8,128)(2,1)}), bf16[1024,768]{1,0:T(8,128)(2,1)}) %all-gather.75.cloned.1.call-update) | async-done | bytes 1572880 | tf_op jit(solution)/shard_map/all_gather | solution.py:80
  361.1 37.6 %all-gather.77.cloned.1.call-done = bf16[1024,768]{1,0:T(8,128)(2,1)} async-done(((bf16[128,768]{1,0:T(8,128)(2,1)}), bf16[1024,768]{1,0:T(8,128)(2,1)}) %all-gather.77.cloned.1.call-update) | async-done | bytes 1572880 | tf_op jit(solution)/shard_map/all_gather | solution.py:81
  408.4 35.2 %all-gather.71.cloned.1.call-done = bf16[1024,768]{1,0:T(8,128)(2,1)} async-done(((bf16[128,768]{1,0:T(8,128)(2,1)}), bf16[1024,768]{1,0:T(8,128)(2,1)}) %all-gather.71.cloned.1.call-update) | async-done | bytes 1572880 | tf_op jit(solution)/shard_map/all_gather | solution.py:80
  452.2 36.6 %all-gather.73.cloned.1.call-done = bf16[1024,768]{1,0:T(8,128)(2,1)} async-done(((bf16[128,768]{1,0:T(8,128)(2,1)}), bf16[1024,768]{1,0:T(8,128)(2,1)}) %all-gather.73.cloned.1.call-update) | async-done | bytes 1572880 | tf_op jit(solution)/shard_map/all_gather | solution.py:81
  499.1 34.8 %all-gather.79.cloned.1.call-done = bf16[1024,768]{1,0:T(8,128)(2,1)} async-done(((bf16[128,768]{1,0:T(8,128)(2,1)}), bf16[1024,768]{1,0:T(8,128)(2,1)}) %all-gather.79.cloned.1.call-update) | async-done | bytes 1572880 | tf_op jit(solution)/shard_map/all_gather | solution.py:80
  542.6 36.4 %all-gather.81.cloned.1.call-done = bf16[1024,768]{1,0:T(8,128)(2,1)} async-done(((bf16[128,768]{1,0:T(8,128)(2,1)}), bf16[1024,768]{1,0:T(8,128)(2,1)}) %all-gather.81.cloned.1.call-update) | async-done | bytes 1572880 | tf_op jit(solution)/shard_map/all_gather | solution.py:81
  589.9 27.8 %all-gather.65.cloned.1.call-done = bf16[768,3072]{1,0:T(8,128)(2,1)} async-done(((bf16[192,3072]{1,0:T(8,128)(2,1)}), bf16[768,3072]{1,0:T(8,128)(2,1)}) %all-gather.65.cloned.1.call-update) | async-done | bytes 4718608 | tf_op jit(solution)/shard_map/all_gather | solution.py:250
  617.8 8.7 multiply_convert_fusion.16
  626.5 30.2 %all-gather.69.cloned.1.call-done = bf16[3072,768]{0,1:T(8,128)(2,1)} async-done(((bf16[768,768]{0,1:T(8,128)(2,1)}), bf16[3072,768]{0,1:T(8,128)(2,1)}) %all-gather.69.cloned.1.call-update) | async-done | bytes 4718608 | tf_op jit(solution)/shard_map/all_gather | solution.py:251
  735.9 7.6 convert_reduce_fusion.21
  745.6 7.7 convert_reduce_fusion.23
  755.3 7.8 convert_reduce_fusion.22
  765.1 8.0 convert_reduce_fusion.20
  778.9 16.7 all_gather.283
  795.6 12.8 all_gather.278
  808.4 15.0 all_gather.273
  823.4 12.9 all_gather.268
  860.2 26.2 %all_gather.284 = f32[1,1024,12]{1,2,0:T(8,128)} all-gather(f32[1,128,12]{1,2,0:T(8,128)S(1)} %copy-done.155), channel_id=1, replica_groups=mesh['dp'=4,'blk'=8] {'blk'}, dimensions={1}, use_global_device_ids=true | all-gather | bytes 55296 | tf_op jit(solution)/shard_map/all_gather | solution.py:151
  886.5 26.1 %all_gather.279 = f32[1,1024,12]{1,2,0:T(8,128)} all-gather(f32[1,128,12]{1,2,0:T(8,128)S(1)} %copy-done.158), channel_id=1, replica_groups=mesh['dp'=4,'blk'=8] {'blk'}, dimensions={1}, use_global_device_ids=true | all-gather | bytes 55296 | tf_op jit(solution)/shard_map/all_gather | solution.py:151
  912.5 26.5 %all_gather.274 = f32[1,1024,12]{1,2,0:T(8,128)} all-gather(f32[1,128,12]{1,2,0:T(8,128)S(1)} %copy-done.156), channel_id=1, replica_groups=mesh['dp'=4,'blk'=8] {'blk'}, dimensions={1}, use_global_device_ids=true | all-gather | bytes 55296 | tf_op jit(solution)/shard_map/all_gather | solution.py:151
  939.0 26.6 %all_gather.269 = f32[1,1024,12]{1,2,0:T(8,128)} all-gather(f32[1,128,12]{1,2,0:T(8,128)S(1)} %copy-done.157), channel_id=1, replica_groups=mesh['dp'=4,'blk'=8] {'blk'}, dimensions={1}, use_global_device_ids=true | all-gather | bytes 55296 | tf_op jit(solution)/shard_map/all_gather | solution.py:151
  982.0 26.5 %all-gather.28 = f32[1024,12]{0,1:T(8,128)} all-gather(f32[128,12]{0,1:T(8,128)S(1)} %copy-done.154), channel_id=30, replica_groups=mesh['dp'=4,'blk'=8] {'blk'}, dimensions={0}, use_global_device_ids=true | all-gather | bytes 55296 | tf_op jit(solution)/shard_map/all_gather | solution.py:152
  1013.2 24.6 %all-gather.25 = f32[1024,12]{0,1:T(8,128)S(1)} all-gather(f32[128,12]{0,1:T(8,128)S(1)} %multiply_reduce_fusion.6), channel_id=27, replica_groups=mesh['dp'=4,'blk'=8] {'blk'}, dimensions={0}, use_global_device_ids=true | all-gather | bytes 55296 | tf_op jit(solution)/shard_map/all_gather | solution.py:152
  1037.8 26.1 %all-gather.22 = f32[1024,12]{0,1:T(8,128)} all-gather(f32[128,12]{0,1:T(8,128)S(1)} %copy-done.152), channel_id=24, replica_groups=mesh['dp'=4,'blk'=8] {'blk'}, dimensions={0}, use_global_device_ids=true | all-gather | bytes 55296 | tf_op jit(solution)/shard_map/all_gather | solution.py:152
  1063.9 24.6 %all-gather.19 = f32[1024,12]{0,1:T(8,128)S(1)} all-gather(f32[128,12]{0,1:T(8,128)S(1)} %copy-done.150), channel_id=21, replica_groups=mesh['dp'=4,'blk'=8] {'blk'}, dimensions={0}, use_global_device_ids=true | all-gather | bytes 55296 | tf_op jit(solution)/shard_map/all_gather | solution.py:152
  1099.3 8.4 fusion.141
  1109.6 8.3 fusion.137
  1119.8 8.7 fusion.139
  1130.3 8.3 fusion.143
  1150.7 6.1 convert_reduce_fusion.19
  1181.2 11.9 add_add_fusion.1
  1207.1 12.4 add_add_fusion
  1234.0 38.4 %reduce-scatter.50.cloned.1.call-done = f32[768,96]{0,1:T(8,128)} async-done(((f32[768,768]{0,1:T(8,128)}), f32[768,96]{0,1:T(8,128)}) %reduce-scatter.50.cloned.1.call-update) | async-done | bytes 294928 | tf_op jit(solution)/shard_map/reduce_scatter | solution.py:265
  1274.4 69.6 %reduce-scatter.52.cloned.1.call-done = f32[768,96]{0,1:T(8,128)} async-done(((f32[768,768]{0,1:T(8,128)}), f32[768,96]{0,1:T(8,128)}) %reduce-scatter.52.cloned.1.call-update) | async-done | bytes 294928 | tf_op jit(solution)/shard_map/reduce_scatter | solution.py:266
  1345.9 165.2 %reduce-scatter.56.cloned.1.call-done = f32[768,384]{1,0:T(8,128)} async-done(((f32[768,3072]{1,0:T(8,128)}), f32[768,384]{1,0:T(8,128)}) %reduce-scatter.56.cloned.1.call-update) | async-done | bytes 1179664 | tf_op jit(solution)/shard_map/reduce_scatter | solution.py:268
  1511.2 62.2 %reduce-scatter.88.cloned.1.call-done = f32[96,1]{1,0:T(8,128)} async-done(((f32[768,1]{1,0:T(8,128)}), f32[96,1]{1,0:T(8,128)}) %reduce-scatter.88.cloned.1.call-update) | async-done | bytes 400
  1578.2 163.2 %reduce-scatter.60.cloned.1.call-done = f32[3072,96]{0,1:T(8,128)} async-done(((f32[3072,768]{0,1:T(8,128)}), f32[3072,96]{0,1:T(8,128)}) %reduce-scatter.60.cloned.1.call-update) | async-done | bytes 1179664 | tf_op jit(solution)/shard_map/reduce_scatter | solution.py:269
  1743.7 59.5 %reduce-scatter.66.cloned.1.call-done = f32[96,1]{1,0:T(8,128)} async-done(((f32[768,1]{1,0:T(8,128)}), f32[96,1]{1,0:T(8,128)}) %reduce-scatter.66.cloned.1.call-update) | async-done | bytes 400
  1804.1 62.7 %reduce-scatter.76.cloned.1.call-done = f32[96,1]{1,0:T(8,128)} async-done(((f32[768,1]{1,0:T(8,128)}), f32[96,1]{1,0:T(8,128)}) %reduce-scatter.76.cloned.1.call-update) | async-done | bytes 400
  1867.7 62.9 %reduce-scatter.78.cloned.1.call-done = f32[96,1]{1,0:T(8,128)} async-done(((f32[768,1]{1,0:T(8,128)}), f32[96,1]{1,0:T(8,128)}) %reduce-scatter.78.cloned.1.call-update) | async-done | bytes 400
  1932.0 62.4 %reduce-scatter.80.cloned.1.call-done = f32[96,1]{1,0:T(8,128)} async-done(((f32[768,1]{1,0:T(8,128)}), f32[96,1]{1,0:T(8,128)}) %reduce-scatter.80.cloned.1.call-update) | async-done | bytes 400
  1995.7 62.2 %reduce-scatter.84.cloned.1.call-done = f32[96,1]{1,0:T(8,128)} async-done(((f32[768,1]{1,0:T(8,128)}), f32[96,1]{1,0:T(8,128)}) %reduce-scatter.84.cloned.1.call-update) | async-done | bytes 400
  2059.3 62.3 %reduce-scatter.86.cloned.1.call-done = f32[96,1]{1,0:T(8,128)} async-done(((f32[768,1]{1,0:T(8,128)}), f32[96,1]{1,0:T(8,128)}) %reduce-scatter.86.cloned.1.call-update) | async-done | bytes 400
  2123.0 66.7 %reduce-scatter.82.cloned.1.call-done = f32[384,1]{1,0:T(8,128)} async-done(((f32[3072,1]{1,0:T(8,128)}), f32[384,1]{1,0:T(8,128)}) %reduce-scatter.82.cloned.1.call-update) | async-done | bytes 1552
  2199.3 53.4 %reduce-scatter.72.cloned.1.call-done = f32[96,1]{1,0:T(8,128)} async-done(((f32[768,1]{1,0:T(8,128)}), f32[96,1]{1,0:T(8,128)}) %reduce-scatter.72.cloned.1.call-update) | async-done | bytes 400
  2253.6 8.3 all-reduce.8
  2261.9 15.9 reduce-scatter.64.cloned.1.call-done
  2277.7 24.1 reduce-scatter.74.cloned.1.call-done
  2301.8 24.1 reduce-scatter.68.cloned.1.call-done
  2325.9 23.9 reduce-scatter.70.cloned.1.call-done
  2349.9 29.1 %reduce-scatter.58.cloned.1.call-done = f32[192,384]{1,0:T(8,128)} async-done(((f32[768,384]{1,0:T(8,128)}), f32[192,384]{1,0:T(8,128)}) %reduce-scatter.58.cloned.1.call-update) | async-done | bytes 294928 | tf_op jit(solution)/shard_map/reduce_scatter | solution.py:285
  2379.0 28.7 %reduce-scatter.62.cloned.1.call-done = f32[768,96]{0,1:T(8,128)} async-done(((f32[3072,96]{0,1:T(8,128)}), f32[768,96]{0,1:T(8,128)}) %reduce-scatter.62.cloned.1.call-update) | async-done | bytes 294928 | tf_op jit(solution)/shard_map/reduce_scatter | solution.py:286
  (875 shorter events, 355.9 us)
Async XLA Ops:
  7.2 82.5 %all-gather.57.cloned.1.call-start = ((), (), s32[]{:S(2)}) async-start(), calls=%async_computation.22 | async-start | bytes 1474560 | tf_op jit(solution)/shard_map/all_gather | solution.py:247
  35.4 89.7 %all-gather.59.cloned.1.call-start = ((), (), s32[]{:S(2)}) async-start(), calls=%async_computation.23 | async-start | bytes 1474560 | tf_op jit(solution)/shard_map/all_gather | solution.py:248
  62.2 98.8 %all-gather.63.cloned.1.call-start = ((), (), s32[]{:S(2)}) async-start(), calls=%async_computation.25 | async-start | bytes 1327104 | tf_op jit(solution)/shard_map/all_gather | solution.py:233
  62.9 116.3 %all-gather.67.cloned.1.call-start = ((), (), s32[]{:S(2)}) async-start(), calls=%async_computation.27 | async-start | bytes 1327104 | tf_op jit(solution)/shard_map/all_gather | solution.py:234
  63.5 134.9 %all-gather.55.cloned.1.call-start = ((), (), s32[]{:S(2)}) async-start(), calls=%async_computation.21 | async-start | bytes 1474560 | tf_op jit(solution)/shard_map/all_gather | solution.py:246
  89.6 204.1 %all-gather.83.cloned.1.call-start = ((), (), s32[]{:S(2)}) async-start(), calls=%async_computation.43 | async-start | bytes 1769472 | tf_op jit(solution)/shard_map/all_gather | solution.py:80
  92.0 207.9 %all-gather.85.cloned.1.call-start = ((), (), s32[]{:S(2)}) async-start(), calls=%async_computation.44 | async-start | bytes 1769472 | tf_op jit(solution)/shard_map/all_gather | solution.py:81
  127.5 180.7 %all-gather.61.cloned.1.call-start = ((), (), s32[]{:S(2)}) async-start(), calls=%async_computation.24 | async-start | bytes 1474560 | tf_op jit(solution)/shard_map/all_gather | solution.py:249
  154.3 199.3 %all-gather.75.cloned.1.call-start = ((), (), s32[]{:S(2)}) async-start(), calls=%async_computation.39 | async-start | bytes 1769472 | tf_op jit(solution)/shard_map/all_gather | solution.py:80
  155.4 243.3 %all-gather.77.cloned.1.call-start = ((), (), s32[]{:S(2)}) async-start(), calls=%async_computation.40 | async-start | bytes 1769472 | tf_op jit(solution)/shard_map/all_gather | solution.py:81
  156.5 287.2 %all-gather.71.cloned.1.call-start = ((), (), s32[]{:S(2)}) async-start(), calls=%async_computation.37 | async-start | bytes 1769472 | tf_op jit(solution)/shard_map/all_gather | solution.py:80
  157.6 331.1 %all-gather.73.cloned.1.call-start = ((), (), s32[]{:S(2)}) async-start(), calls=%async_computation.38 | async-start | bytes 1769472 | tf_op jit(solution)/shard_map/all_gather | solution.py:81
  158.7 375.3 %all-gather.79.cloned.1.call-start = ((), (), s32[]{:S(2)}) async-start(), calls=%async_computation.41 | async-start | bytes 1769472 | tf_op jit(solution)/shard_map/all_gather | solution.py:80
  159.8 419.3 %all-gather.81.cloned.1.call-start = ((), (), s32[]{:S(2)}) async-start(), calls=%async_computation.42 | async-start | bytes 1769472 | tf_op jit(solution)/shard_map/all_gather | solution.py:81
  160.9 456.9 %all-gather.65.cloned.1.call-start = ((), (), s32[]{:S(2)}) async-start(), calls=%async_computation.26 | async-start | bytes 5898240 | tf_op jit(solution)/shard_map/all_gather | solution.py:250
  161.5 495.2 %all-gather.69.cloned.1.call-start = ((), (), s32[]{:S(2)}) async-start(), calls=%async_computation.28 | async-start | bytes 5898240 | tf_op jit(solution)/shard_map/all_gather | solution.py:251
  179.3 670.4 %all-gather.99.cloned.1.call-start = ((), (), s32[]{:S(2)}) async-start(), calls=%async_computation.51 | async-start | bytes 1769472 | tf_op jit(solution)/shard_map/all_gather | solution.py:149
  200.9 651.4 %all-gather.95.cloned.1.call-start = ((), (), s32[]{:S(2)}) async-start(), calls=%async_computation.49 | async-start | bytes 1769472 | tf_op jit(solution)/shard_map/all_gather | solution.py:149
  201.9 86.8 %copy-start.57 = (bf16[128,768]{1,0:T(8,128)(2,1)S(1)}, bf16[128,768]{1,0:T(8,128)(2,1)}, u32[]{:S(2)}) copy-start(bf16[128,768]{1,0:T(8,128)(2,1)} %fusion.150) | copy-start | bytes 589828
  202.0 89.4 %copy-start.58 = (bf16[128,768]{1,0:T(8,128)(2,1)S(1)}, bf16[128,768]{1,0:T(8,128)(2,1)}, u32[]{:S(2)}) copy-start(bf16[128,768]{1,0:T(8,128)(2,1)} %fusion.148) | copy-start | bytes 589828
  202.0 652.9 %all-gather.91.cloned.1.call-start = ((), (), s32[]{:S(2)}) async-start(), calls=%async_computation.47 | async-start | bytes 1769472 | tf_op jit(solution)/shard_map/all_gather | solution.py:149
  203.1 654.4 %all-gather.87.cloned.1.call-start = ((), (), s32[]{:S(2)}) async-start(), calls=%async_computation.45 | async-start | bytes 1769472 | tf_op jit(solution)/shard_map/all_gather | solution.py:149
  226.1 271.1 %copy-start.132 = (f32[768]{0:T(1024)}, f32[768]{0:T(1024)S(1)}, u32[]{:S(2)}) copy-start(f32[768]{0:T(1024)S(1)} %add.1249) | copy-start | bytes 9220
  288.3 112.9 %copy-start.69 = (pred[128,1024]{1,0:T(8,128)(4,1)}, pred[128,1024]{1,0:T(8,128)(4,1)S(1)}, u32[]{:S(2)}) copy-start(pred[128,1024]{1,0:T(8,128)(4,1)S(1)} %compare_reduce_fusion.6) | copy-start | bytes 393220
  288.5 202.8 %copy-start.71 = (pred[128,1024]{1,0:T(8,128)(4,1)}, pred[128,1024]{1,0:T(8,128)(4,1)S(1)}, u32[]{:S(2)}) copy-start(pred[128,1024]{1,0:T(8,128)(4,1)S(1)} %compare_reduce_fusion.7) | copy-start | bytes 393220
  288.8 292.9 %copy-start.73 = (pred[128,1024]{1,0:T(8,128)(4,1)}, pred[128,1024]{1,0:T(8,128)(4,1)S(1)}, u32[]{:S(2)}) copy-start(pred[128,1024]{1,0:T(8,128)(4,1)S(1)} %compare_reduce_fusion.5) | copy-start | bytes 393220
  293.3 795.2 %all-gather.101.cloned.1.call-start = ((), (), s32[]{:S(2)}) async-start(), calls=%async_computation.52 | async-start | bytes 1769472 | tf_op jit(solution)/shard_map/all_gather | solution.py:150
  708.8 382.3 %all-gather.97.cloned.1.call-start = ((), (), s32[]{:S(2)}) async-start(), calls=%async_computation.50 | async-start | bytes 1769472 | tf_op jit(solution)/shard_map/all_gather | solution.py:150
  711.1 382.6 %all-gather.93.cloned.1.call-start = ((), (), s32[]{:S(2)}) async-start(), calls=%async_computation.48 | async-start | bytes 1769472 | tf_op jit(solution)/shard_map/all_gather | solution.py:150
  713.4 383.0 %all-gather.89.cloned.1.call-start = ((), (), s32[]{:S(2)}) async-start(), calls=%async_computation.46 | async-start | bytes 1769472 | tf_op jit(solution)/shard_map/all_gather | solution.py:150
  734.5 495.5 %reduce-scatter.48.cloned.1.call-start = ((), (), s32[]{:S(2)}) async-start(), calls=%async_computation.29 | async-start | bytes 2654208 | tf_op jit(solution)/shard_map/reduce_scatter | solution.py:264
  778.3 69.5 %copy-start.54 = (bf16[128,768]{1,0:T(8,128)(2,1)S(1)}, bf16[128,768]{1,0:T(8,128)(2,1)}, u32[]{:S(2)}) copy-start(bf16[128,768]{1,0:T(8,128)(2,1)} %fusion.147) | copy-start | bytes 589828
  778.3 70.3 %copy-start.55 = (bf16[128,768]{1,0:T(8,128)(2,1)S(1)}, bf16[128,768]{1,0:T(8,128)(2,1)}, u32[]{:S(2)}) copy-start(bf16[128,768]{1,0:T(8,128)(2,1)} %convolution_convert_fusion.7) | copy-start | bytes 589828
  778.3 453.7 %reduce-scatter.54.cloned.1.call-start = ((), (), s32[]{:S(2)}) async-start(), calls=%async_computation.32 | async-start | bytes 2654208 | tf_op jit(solution)/shard_map/reduce_scatter | solution.py:267
  857.5 81.5 %copy-start.157 = (f32[1,128,12]{1,2,0:T(8,128)S(1)}, f32[1,128,12]{1,2,0:T(8,128)}, u32[]{:S(2)}) copy-start(f32[1,128,12]{1,2,0:T(8,128)} %get-tuple-element.214) | copy-start | bytes 18436
  857.5 108.1 %copy-start.101 = (bf16[128,768]{0,1:T(8,128)(2,1)S(1)}, bf16[128,768]{0,1:T(8,128)(2,1)}, u32[]{:S(2)}) copy-start(bf16[128,768]{0,1:T(8,128)(2,1)} %copy.312) | copy-start | bytes 589828
  1013.2 259.3 %reduce-scatter.50.cloned.1.call-start = ((), (), s32[]{:S(2)}) async-start(), calls=%async_computation.30 | async-start | bytes 2654208 | tf_op jit(solution)/shard_map/reduce_scatter | solution.py:265
  1143.7 200.3 %reduce-scatter.52.cloned.1.call-start = ((), (), s32[]{:S(2)}) async-start(), calls=%async_computation.31 | async-start | bytes 2654208 | tf_op jit(solution)/shard_map/reduce_scatter | solution.py:266
  1168.2 342.9 %reduce-scatter.56.cloned.1.call-start = ((), (), s32[]{:S(2)}) async-start(), calls=%async_computation.33 | async-start | bytes 10616832 | tf_op jit(solution)/shard_map/reduce_scatter | solution.py:268
  1193.2 380.3 %reduce-scatter.88.cloned.1.call-start = ((), (), s32[]{:S(2)}) async-start(), calls=%async_computation.65 | async-start | bytes 442368
  1195.4 546.0 %reduce-scatter.60.cloned.1.call-start = ((), (), s32[]{:S(2)}) async-start(), calls=%async_computation.35 | async-start | bytes 10616832 | tf_op jit(solution)/shard_map/reduce_scatter | solution.py:269
  1219.6 583.6 %reduce-scatter.66.cloned.1.call-start = ((), (), s32[]{:S(2)}) async-start(), calls=%async_computation.54 | async-start | bytes 442368
  1221.3 645.5 %reduce-scatter.76.cloned.1.call-start = ((), (), s32[]{:S(2)}) async-start(), calls=%async_computation.59 | async-start | bytes 442368
  1222.5 708.1 %reduce-scatter.78.cloned.1.call-start = ((), (), s32[]{:S(2)}) async-start(), calls=%async_computation.60 | async-start | bytes 442368
  1223.6 770.8 %reduce-scatter.80.cloned.1.call-start = ((), (), s32[]{:S(2)}) async-start(), calls=%async_computation.61 | async-start | bytes 442368
  1224.6 833.3 %reduce-scatter.84.cloned.1.call-start = ((), (), s32[]{:S(2)}) async-start(), calls=%async_computation.63 | async-start | bytes 442368
  1225.9 895.7 %reduce-scatter.86.cloned.1.call-start = ((), (), s32[]{:S(2)}) async-start(), calls=%async_computation.64 | async-start | bytes 442368
  1226.9 962.7 %reduce-scatter.82.cloned.1.call-start = ((), (), s32[]{:S(2)}) async-start(), calls=%async_computation.62 | async-start | bytes 1769472
  1228.7 1024.0 %reduce-scatter.72.cloned.1.call-start = ((), (), s32[]{:S(2)}) async-start(), calls=%async_computation.57 | async-start | bytes 442368
  1229.9 1047.8 %reduce-scatter.64.cloned.1.call-start = ((), (), s32[]{:S(2)}) async-start(), calls=%async_computation.53 | async-start | bytes 491520
  1231.9 1069.9 %reduce-scatter.74.cloned.1.call-start = ((), (), s32[]{:S(2)}) async-start(), calls=%async_computation.58 | async-start | bytes 491520
  1233.9 340.4 %copy-start.75 = (bf16[1,1,128,768]{3,2,1,0:T(8,128)(2,1)S(1)}, bf16[1,1,128,768]{3,2,1,0:T(8,128)(2,1)}, u32[]{:S(2)}) copy-start(bf16[1,1,128,768]{3,2,1,0:T(8,128)(2,1)} %get-tuple-element.212) | copy-start | bytes 589828
  1233.9 340.4 %copy-start.76 = (bf16[1,1,128,768]{3,2,1,0:T(8,128)(2,1)S(1)}, bf16[1,1,128,768]{3,2,1,0:T(8,128)(2,1)}, u32[]{:S(2)}) copy-start(bf16[1,1,128,768]{3,2,1,0:T(8,128)(2,1)} %get-tuple-element.213) | copy-start | bytes 589828
  1233.9 340.4 %copy-start.77 = (bf16[1,1,128,768]{3,2,1,0:T(8,128)(2,1)S(1)}, bf16[1,1,128,768]{3,2,1,0:T(8,128)(2,1)}, u32[]{:S(2)}) copy-start(bf16[1,1,128,768]{3,2,1,0:T(8,128)(2,1)} %get-tuple-element.210) | copy-start | bytes 589828
  1234.0 340.4 %copy-start.78 = (bf16[1,1,128,768]{3,2,1,0:T(8,128)(2,1)S(1)}, bf16[1,1,128,768]{3,2,1,0:T(8,128)(2,1)}, u32[]{:S(2)}) copy-start(bf16[1,1,128,768]{3,2,1,0:T(8,128)(2,1)} %get-tuple-element.211) | copy-start | bytes 589828
  1234.0 1092.0 %reduce-scatter.68.cloned.1.call-start = ((), (), s32[]{:S(2)}) async-start(), calls=%async_computation.55 | async-start | bytes 491520
  1274.4 1075.5 %reduce-scatter.70.cloned.1.call-start = ((), (), s32[]{:S(2)}) async-start(), calls=%async_computation.56 | async-start | bytes 491520
  1345.9 229.5 %copy-start.6 = (bf16[768,768]{1,0:T(8,128)(2,1)S(1)}, bf16[768,768]{1,0:T(8,128)(2,1)}, u32[]{:S(2)}) copy-start(bf16[768,768]{1,0:T(8,128)(2,1)} %all-gather.55.cloned.1.call-done) | copy-start | bytes 3538948
  1345.9 229.5 %copy-start.91 = (bf16[12,64,128]{2,1,0:T(8,128)(2,1)S(1)}, bf16[12,64,128]{2,1,0:T(8,128)(2,1)}, u32[]{:S(2)}) copy-start(bf16[12,64,128]{2,1,0:T(8,128)(2,1)} %copy-done.90) | copy-start | bytes 589828
  1345.9 1033.1 %reduce-scatter.58.cloned.1.call-start = ((), (), s32[]{:S(2)}) async-start(), calls=%async_computation.34 | async-start | bytes 1474560 | tf_op jit(solution)/shard_map/reduce_scatter | solution.py:285
  1511.2 896.5 %reduce-scatter.62.cloned.1.call-start = ((), (), s32[]{:S(2)}) async-start(), calls=%async_computation.36 | async-start | bytes 1474560 | tf_op jit(solution)/shard_map/reduce_scatter | solution.py:286
  1577.7 163.7 %copy-start.16 = (f32[128,768]{1,0:T(8,128)S(1)}, f32[128,768]{1,0:T(8,128)}, u32[]{:S(2)}) copy-start(f32[128,768]{1,0:T(8,128)} %get-tuple-element.166) | copy-start | bytes 1179652
  1741.4 449.3 %copy-start.2 = (bf16[768,768]{1,0:T(8,128)(2,1)S(1)}, bf16[768,768]{1,0:T(8,128)(2,1)}, u32[]{:S(2)}) copy-start(bf16[768,768]{1,0:T(8,128)(2,1)} %all-gather.57.cloned.1.call-done) | copy-start | bytes 3538948
  1743.7 448.7 %copy-start.4 = (bf16[768,768]{1,0:T(8,128)(2,1)S(1)}, bf16[768,768]{1,0:T(8,128)(2,1)}, u32[]{:S(2)}) copy-start(bf16[768,768]{1,0:T(8,128)(2,1)} %all-gather.59.cloned.1.call-done) | copy-start | bytes 3538948
  (228 other events, 2354.0 us)
Sparse Core Ops, SparseCore 0:
  35.5 24.8 all-gather.56
  62.5 30.7 all-gather.58
  95.4 38.4 all-gather.62
  135.9 43.3 all-gather.66
  181.2 17.1 all-gather.54
  200.4 43.2 all-gather.82
  245.9 42.8 all-gather.84
  290.9 17.2 all-gather.60
  310.4 43.1 all-gather.74
  355.7 42.9 all-gather.76
  400.9 42.7 all-gather.70
  445.7 42.9 all-gather.72
  490.9 42.9 all-gather.78
  536.0 42.9 all-gather.80
  580.4 37.2 all-gather.64
  619.2 37.4 all-gather.68
  659.3 43.1 all-gather.98
  704.5 42.9 all-gather.94
  749.7 43.0 all-gather.90
  794.9 42.7 all-gather.86
  839.9 43.2 all-gather.100
  885.3 43.0 all-gather.96
  930.7 43.2 all-gather.92
  976.0 42.9 all-gather.88
  1022.5 68.2 reduce-scatter.47
  1094.1 68.1 reduce-scatter.53
  1165.6 106.7 reduce-scatter.49
  1275.9 68.0 reduce-scatter.51
  1347.6 163.5 reduce-scatter.55
  1514.8 58.5 reduce-scatter.87
  1577.0 164.2 reduce-scatter.59
  1744.6 58.5 reduce-scatter.65
  1806.3 60.4 reduce-scatter.75
  1870.1 60.4 reduce-scatter.77
  1933.8 60.4 reduce-scatter.79
  1997.4 60.4 reduce-scatter.83
  2061.1 60.4 reduce-scatter.85
  2125.0 64.6 reduce-scatter.81
  2193.1 59.5 reduce-scatter.71
  2255.9 21.7 reduce-scatter.63
  2281.0 20.8 reduce-scatter.73
  2305.1 20.8 reduce-scatter.67
  2329.0 20.8 reduce-scatter.69
  2353.2 25.7 reduce-scatter.57
  2382.0 25.7 reduce-scatter.61
where the time goes:
time: 2430 us; the launch traced here: 2410 us
  waiting for transfers between devices  1460 us (60%)
  blocking collectives  482 us (20%)
  matrix products  294 us (12%)
  local copies, waits for them, and re-layouts  116 us (5%)
  other arithmetic  43.9 us (2%)
    unnamed x58, waiting for transfers between devices  645 us
    dot_general x96, matrix products, product(): return jnp.einsum(form, left, right, preferred_element_type=jnp.float32)  294 us
    reduce_scatter x1, waiting for transfers between devices, on_device(): lax.psum_scatter(totals[4], 'blk', scatter_dimension=1, tiled=True)  165 us
    reduce_scatter x1, waiting for transfers between devices, on_device(): lax.psum_scatter(totals[5], 'blk', scatter_dimension=1, tiled=True)  163 us
    all_gather x4, waiting for transfers between devices, micro_step(): key_piece = lax.all_gather(key_rows, 'blk', axis=1, tiled=True)  113 us
    all_gather x4, waiting for transfers between devices, micro_step(): value_piece = lax.all_gather(value_rows, 'blk', axis=1, tiled=True)  111 us
    all_gather x4, blocking collectives, micro_step(): total_piece = lax.all_gather(sent[2], 'blk', axis=1, tiled=True)  105 us
    all_gather x4, blocking collectives, micro_step(): delta_piece = lax.all_gather(sent[3], 'blk', axis=1, tiled=True)  102 us
  transfers between devices with their start and end apart: 45, of which 30 were waited for; matrix products, arithmetic and copies ran while one was open for 18% of the time, Pallas kernels for 0%

commit v1 on v0

--- a/solution.py
+++ b/solution.py
@@ -3,10 +3,706 @@
 import jax
 import jax.numpy as jnp
 from jax import lax
+from jax.experimental import pallas as pl
+from jax.experimental.pallas import tpu as pltpu
 from jax.sharding import PartitionSpec as P
 
-HEADS = 12
-HD = 64
+MESH = pl.DeviceIdType.MESH
+BF = jnp.bfloat16
+F32 = jnp.float32
+
+
+def place():
+    dp = lax.axis_index("dp")
+    blk = lax.axis_index("blk")
+    return dp // 2, dp % 2, blk // 2, blk % 2
+
+
+def device(y, c, z, x):
+    return (y * 2 + c, z * 2 + x)
+
+
+def greet_all():
+    y, c, z, x = place()
+    me = (y * 2 + c) * 8 + z * 2 + x
+    barrier = pltpu.get_barrier_semaphore()
+
+    def greet(i, carry):
+        other = (me + i) % 32
+        pl.semaphore_signal(barrier, inc=1, device_id=(other // 8, other % 8), device_id_type=MESH)
+        return carry
+
+    lax.fori_loop(1, 32, greet, 0)
+    pl.semaphore_wait(barrier, 31)
+
+
+XY, YX = "abxyc", "abyxc"
+CHUNKS = [("t", 0, XY), ("t", 1, YX), ("t", 2, XY), ("t", 3, YX)]
+for _i in range(4):
+    CHUNKS += [("u", _i, XY), ("d", _i, YX)]
+OFF = (1, 2, 4, 6, 7)
+XT = 5
+
+
+def coords():
+    y, c, z, x = place()
+    return {"a": z // 2, "b": z % 2, "x": x, "y": y, "c": c}
+
+
+def to_device(at):
+    return device(at["y"], at["c"], 2 * at["a"] + at["b"], at["x"])
+
+
+def flip(at, dim):
+    return {**at, dim: 1 - at[dim]}
+
+
+def whole(at, dims):
+    return {k: (None if k in dims else v) for k, v in at.items()}
+
+
+def span(v):
+    return slice(None) if v is None else v
+
+
+def each(v):
+    return (0, 1) if v is None else (v,)
+
+
+def lanes(start, size):
+    return pl.ds(start if isinstance(start, int) else pl.multiple_of(start, 128), size)
+
+
+def region(refs, chunk, at):
+    wt, wu, wd = refs
+    kind, i, _ = chunk
+    a, b, x, y, c = (at[k] for k in "abxyc")
+    if kind == "t":
+        cols = slice(None) if y is None else lanes(384 * y, 384)
+        return [wt.at[i, span(a), span(b), span(x), span(c), :, cols]]
+    if kind == "u":
+        if a is None and b is None and x is None:
+            return [wu.at[span(y), span(c), i]]
+        return [wu.at[span(y), span(c), i, :, lanes(384 * (4 * p + 2 * q + r), 384)] for p in each(a) for q in each(b) for r in each(x)]
+    return [wd.at[span(a), span(b), span(x), i // 2, :, lanes(768 * (2 * p + q) + 384 * (i % 2), 384)] for p in each(y) for q in each(c)]
+
+
+def gather_kernel(
+    xs, cot, seg, w4, wup, wdt, vec,
+    X, C, SEG, WT, WUP, WDT, VEC,
+    pair, stage,
+    ps, pr, zs, zr, ls, xsnd, xrcv, xfs, xfr, csnd, crcv, ssnd, srcv, vsnd, vrcv, lsem,
+):
+    y, c, z, x = place()
+    j = 2 * z + x
+    greet_all()
+    sends = []
+
+    def remote(src, dst, send, recv, to, start=True):
+        cp = pltpu.make_async_remote_copy(src_ref=src, dst_ref=dst, send_sem=send, recv_sem=recv, device_id=to, device_id_type=MESH)
+        if start is True:
+            cp.start()
+        else:
+            pl.when(start)(cp.start)
+        sends.append((start, cp))
+        return cp
+
+    def arrive(dst, recv):
+        pltpu.make_async_remote_copy(src_ref=dst, dst_ref=dst, send_sem=recv, recv_sem=recv, device_id=device(y, c, z, x), device_id_type=MESH).wait_recv()
+
+    partner = device(y, 1 - c, z, x)
+    first = remote(w4.at[:, pl.ds(48 * (1 - c), 48)], pair, ps, pr, partner)
+
+    def tokens(src, dst, i, send, recv, loc):
+        m = (z + i) % 4
+        to = device(y, z // 2, m, c)
+        mine = (z == m) & (x == c) & (z // 2 == c)
+        cp = pltpu.make_async_remote_copy(src_ref=src.at[m], dst_ref=dst, send_sem=send, recv_sem=recv, device_id=to, device_id_type=MESH)
+        lc = pltpu.make_async_copy(src.at[m], dst, loc)
+        pl.when(jnp.logical_not(mine))(cp.start)
+        pl.when(mine)(lc.start)
+        return mine, cp, lc
+
+    conds = []
+    for m in range(4):
+        conds.append(tokens(xs, X.at[j], m, xsnd.at[m], xrcv.at[j % 4], lsem.at[0]))
+    for m in range(4):
+        for k in range(2):
+            to = device(y, k, m, c)
+            mine = (z == m) & (x == c) & (k == c)
+            cp = pltpu.make_async_remote_copy(src_ref=seg.at[m], dst_ref=SEG.at[j], send_sem=ssnd.at[2 * m + k], recv_sem=srcv.at[j], device_id=to, device_id_type=MESH)
+            lc = pltpu.make_async_copy(seg.at[m], SEG.at[j], lsem.at[1])
+            pl.when(jnp.logical_not(mine))(cp.start)
+            pl.when(mine)(lc.start)
+            conds.append((mine, cp, lc))
+    own_vec = pltpu.make_async_copy(vec, VEC.at[j], lsem.at[2])
+    own_vec.start()
+    for d in range(1, 8):
+        o = (j + d) % 8
+        remote(vec, VEC.at[j], vsnd.at[d], vrcv.at[d], device(y, c, o // 2, o % 2))
+
+    first.wait_recv()
+    own = w4[:, pl.ds(pl.multiple_of(48 * c, 16), 48), :]
+    got = pair[...]
+    lo = jnp.where(c == 0, own, got)
+    hi = jnp.where(c == 0, got, own)
+    stage[...] = jnp.concatenate([lo, hi], axis=-1)
+
+    def source(ch):
+        kind, i, _ = ch
+        if kind == "t":
+            return stage.at[i]
+        if kind == "u":
+            return wup.at[i]
+        return wdt.at[i // 2, :, pl.ds(384 * (i % 2), 384)]
+
+    at = coords()
+    refs = (WT, WUP, WDT)
+    n = len(CHUNKS)
+    locals_ = []
+    for t in range(n + OFF[4]):
+        if t < n:
+            ch = CHUNKS[t]
+            here = region(refs, ch, at)[0]
+            lc = pltpu.make_async_copy(source(ch), here, ls.at[t])
+            lc.start()
+            locals_.append(lc)
+            remote(source(ch), here, zs.at[t, 0, 0], zr.at[t, 0, 0], to_device(flip(at, ch[2][0])))
+        if t == XT:
+            for i in range(4):
+                b = 4 * c + i
+                is_mine = (b // 2 == z) & (b % 2 == x) & (c == x)
+
+                @pl.when(jnp.logical_not(is_mine))
+                def _(b=b, i=i):
+                    arrive(X.at[b], xrcv.at[i])
+
+                @pl.when(is_mine)
+                def _(b=b):
+                    pltpu.make_async_copy(X.at[b], X.at[b], lsem.at[0]).wait()
+
+                remote(X.at[b], X.at[b], xfs.at[i], xfr.at[i], partner)
+        if t in (4, 6, 8, 10):
+            m = (t - 4) // 2
+            conds.append(tokens(cot, C.at[j % 4], m, csnd.at[m], crcv.at[j % 4], lsem.at[3]))
+        for s in range(5):
+            u = t - OFF[s]
+            if not 0 <= u < n:
+                continue
+            ch = CHUNKS[u]
+            order = ch[2]
+            if s == 0:
+                locals_[u].wait()
+            for k, part in enumerate(region(refs, ch, whole(flip(at, order[s]), order[:s]))):
+                arrive(part, zr.at[u, s, k])
+            if s < 4:
+                for k, part in enumerate(region(refs, ch, whole(at, order[: s + 1]))):
+                    remote(part, part, zs.at[u, s + 1, k], zr.at[u, s + 1, k], to_device(flip(at, order[s + 1])))
+    for i in range(4):
+        b = 4 * (1 - c) + i
+        arrive(X.at[b], xfr.at[i])
+        b = 4 * c + i
+        is_mine = (b // 2 == z) & (b % 2 == x) & (c == x)
+
+        @pl.when(jnp.logical_not(is_mine))
+        def _(i=i):
+            arrive(C.at[i], crcv.at[i])
+
+        @pl.when(is_mine)
+        def _(i=i):
+            pltpu.make_async_copy(C.at[i], C.at[i], lsem.at[3]).wait()
+    for b in range(8):
+        is_mine = (b // 2 == z) & (b % 2 == x) & (c == x)
+
+        @pl.when(jnp.logical_not(is_mine))
+        def _(b=b):
+            arrive(SEG.at[b], srcv.at[b])
+
+        @pl.when(is_mine)
+        def _(b=b):
+            pltpu.make_async_copy(SEG.at[b], SEG.at[b], lsem.at[1]).wait()
+    own_vec.wait()
+    for d in range(1, 8):
+        arrive(VEC.at[(j - d) % 8], vrcv.at[d])
+    for cond, cp in sends:
+        if cond is True:
+            cp.wait_send()
+        else:
+            pl.when(cond)(cp.wait_send)
+    for mine, cp, lc in conds:
+        pl.when(jnp.logical_not(mine))(cp.wait_send)
+
+
+def gather_call(xs, cot, seg, w4, wup, wdt, vec):
+    any_ = pl.BlockSpec(memory_space=pl.ANY)
+    vm = pl.BlockSpec(memory_space=pltpu.VMEM)
+    n = len(CHUNKS)
+    S = pltpu.SemaphoreType.DMA
+    return pl.pallas_call(
+        gather_kernel,
+        out_shape=[
+            jax.ShapeDtypeStruct((8, 128, 768), BF),
+            jax.ShapeDtypeStruct((4, 128, 768), BF),
+            jax.ShapeDtypeStruct((8, 1, 128), jnp.int32),
+            jax.ShapeDtypeStruct((4, 2, 2, 2, 2, 48, 768), BF),
+            jax.ShapeDtypeStruct((2, 2, 4, 48, 3072), BF),
+            jax.ShapeDtypeStruct((2, 2, 2, 2, 48, 3072), BF),
+            jax.ShapeDtypeStruct((8, 16, 384), BF),
+        ],
+        in_specs=[any_, any_, vm, vm, vm, vm, vm],
+        out_specs=[any_] * 7,
+        scratch_shapes=[
+            pltpu.VMEM((4, 48, 192), BF),
+            pltpu.VMEM((4, 48, 384), BF),
+            S, S, S((n, 5, 4)), S((n, 5, 4)), S((n,)),
+            S((4,)), S((4,)), S((4,)), S((4,)), S((4,)), S((4,)), S((8,)), S((8,)), S((8,)), S((8,)), S((4,)),
+        ],
+        name="gather",
+        compiler_params=pltpu.CompilerParams(collective_id=1, has_side_effects=True, vmem_limit_bytes=48 * 2**20),
+    )(xs, cot, seg, w4, wup, wdt, vec)
+
+
+def prepare(a):
+    (inputs, segment_ids, query_weight, query_bias, key_weight, value_weight, value_bias, output_weight, output_bias,
+     first_gain, first_shift, up_weight, up_bias, down_weight, down_bias, second_gain, second_shift, cotangent) = a
+    w4 = jnp.stack([query_weight, key_weight, value_weight, output_weight]).swapaxes(1, 2)
+    wup = up_weight.reshape(4, 48, 384)
+    wdt = down_weight.T.reshape(2, 48, 768)
+    small = jnp.stack([query_bias, value_bias, output_bias, first_gain, first_shift, down_bias, second_gain, second_shift])
+    small = jnp.pad(small, ((0, 0), (0, 288)))
+    vec = jnp.concatenate([small, up_bias[None], jnp.zeros((7, 384), BF)])
+    return inputs.reshape(4, 128, 768), cotangent.reshape(4, 128, 768), segment_ids.reshape(4, 1, 128), w4, wup, wdt, vec
+
+
+HEADS, HD = 12, 64
+NT = (((1,), (1,)), ((), ()))
+NN = (((1,), (0,)), ((), ()))
+
+
+def dot(l, r, dims=NN):
+    return lax.dot_general(l, r, dims, preferred_element_type=F32)
+
+
+def vector(VEC, i):
+    return jnp.concatenate([VEC[j, pl.ds(i, 1), :][:, :96] for j in range(8)], axis=-1).astype(F32)
+
+
+def attend_kernel(X, WT, SEG, VEC, Q, KT, V, E, CT, RS, kbuf, vtbuf, mask, sbuf, ebuf, esem):
+    _, c, _, _ = place()
+    own = X[pl.ds(pl.multiple_of(512 * c, 128), 512), :]
+    q = dot(own, WT[0], NT) + vector(VEC, 0)
+    Q[...] = (q.astype(BF).astype(F32) * 0.125).astype(BF)
+    k = dot(X[...], WT[1], NT)
+    kbuf[...] = k.astype(BF)
+    KT[...] = k.T.astype(BF)
+    v = dot(X[...], WT[2], NT) + vector(VEC, 1)
+    V[...] = v.astype(BF)
+    vtbuf[...] = v.T.astype(BF)
+    row = jnp.concatenate([SEG[j] for j in range(8)], axis=-1).astype(F32)
+    mine = jnp.concatenate([SEG[4 * c + j] for j in range(4)], axis=-1).astype(F32)
+    col = jnp.broadcast_to(row, (8, 1024)).T[:, :1]
+    mask[...] = jnp.where(col == mine, 0.0, -1e30)
+
+    def pair(p, carry):
+        lanes = pl.ds(pl.multiple_of(128 * p, 128), 128)
+        kp = kbuf[:, lanes]
+        qp = Q[:, lanes]
+        half = lax.broadcasted_iota(jnp.int32, (512, 128), 1) // 64
+        for i in range(2):
+            h = 2 * p + i
+            qm = jnp.where(half == i, qp, jnp.zeros_like(qp))
+            s = dot(kp, qm, NT) + mask[...]
+            m = jnp.max(s, axis=0, keepdims=True)
+            e = jnp.exp(s - m)
+            r = 1.0 / jnp.sum(e, axis=0, keepdims=True)
+
+            @pl.when(p > 0)
+            def _():
+                pltpu.make_async_copy(ebuf.at[i], E.at[h], esem.at[i]).wait()
+
+            ebuf[i] = e.astype(BF)
+            pltpu.make_async_copy(ebuf.at[i], E.at[h], esem.at[i]).start()
+            RS[pl.ds(h, 1), :] = r
+            rows = pl.ds(pl.multiple_of(64 * h, 64), 64)
+            CT[rows, :] = (dot(vtbuf[rows, :], ebuf[i]) * r).astype(BF)
+        return carry
+
+    lax.fori_loop(0, 6, pair, 0)
+    for i in range(2):
+        pltpu.make_async_copy(ebuf.at[i], E.at[10 + i], esem.at[i]).wait()
+
+
+VM = pl.BlockSpec(memory_space=pltpu.VMEM)
+ANY = pl.BlockSpec(memory_space=pl.ANY)
+
+
+def sds(shape, dt=BF):
+    return jax.ShapeDtypeStruct(shape, dt)
+
+
+def attend_call(X, WT, SEG, VEC):
+    return pl.pallas_call(
+        attend_kernel,
+        out_shape=[sds((512, 768)), sds((768, 1024)), sds((1024, 768)), sds((12, 1024, 512)), sds((768, 512)), sds((16, 512), F32)],
+        in_specs=[VM] * 4,
+        out_specs=[VM, VM, VM, ANY, VM, VM],
+        scratch_shapes=[pltpu.VMEM((1024, 768), BF), pltpu.VMEM((768, 1024), BF), pltpu.VMEM((1024, 512), F32), pltpu.VMEM((8, 128), F32), pltpu.VMEM((2, 1024, 512), BF), pltpu.SemaphoreType.DMA((2,))],
+        name="attend",
+        compiler_params=pltpu.CompilerParams(vmem_limit_bytes=56 * 2**20),
+    )(X, WT, SEG, VEC)
+
+
+def norm(h):
+    centred = h - jnp.mean(h, axis=-1, keepdims=True)
+    inv = lax.rsqrt(jnp.mean(centred * centred, axis=-1, keepdims=True) + 1e-12)
+    return centred * inv, inv
+
+
+def norm_back(g, normed, inv):
+    return inv * (g - jnp.mean(g, axis=-1, keepdims=True) - normed * jnp.mean(g * normed, axis=-1, keepdims=True))
+
+
+FC = 768
+
+
+def feed_kernel(X, CT, WO, WU, WD, VEC, COT, OUT, GF, GC, GO, GU, GD, VS, hid, dge, acc, acc2):
+    _, c, _, _ = place()
+    x = X[pl.ds(pl.multiple_of(512 * c, 128), 512), :].astype(F32)
+    ctx = CT[...].astype(F32).T.astype(BF)
+    h = x + dot(ctx, WO[...], NT) + vector(VEC, 2)
+    normed1, inv1 = norm(h)
+    gain1 = vector(VEC, 3)
+    first = normed1 * gain1 + vector(VEC, 4)
+    low = first.astype(BF)
+    upb = jnp.concatenate([VEC[j, pl.ds(8, 1), :] for j in range(8)], axis=-1).astype(F32)
+    for f in range(3072 // FC):
+        cols = slice(FC * f, FC * (f + 1))
+        inner = dot(low, WU[:, cols]) + upb[:, cols]
+        cdf = 0.5 * (1.0 + lax.erf(inner * 0.7071067811865476))
+        pdf = jnp.exp(-0.5 * inner * inner) * 0.3989422804014327
+        hid[:, cols] = (inner * cdf).astype(BF)
+        dge[:, cols] = (cdf + inner * pdf).astype(BF)
+        part = dot(hid[:, cols], WD[:, cols], NT)
+        if f == 0:
+            acc[...] = part
+        else:
+            acc[...] += part
+    normed2, inv2 = norm(first + acc[...] + vector(VEC, 5))
+    gain2 = vector(VEC, 6)
+    OUT[...] = (normed2 * gain2 + vector(VEC, 7)).astype(BF)
+    up = COT[...].astype(F32)
+
+    def total(v):
+        return jnp.sum(v, axis=0, keepdims=True)
+
+    VS[...] = jnp.zeros_like(VS)
+    VS[6:7, :768] = total(up * normed2)
+    VS[7:8, :768] = total(up)
+    gss = norm_back(up * gain2, normed2, inv2)
+    gs = gss.astype(BF)
+    VS[5:6, :768] = total(gs.astype(F32))
+    gst = gss.T.astype(BF)
+    lowt = first.T.astype(BF)
+    acc2[...] = gss
+    for f in range(3072 // FC):
+        cols = slice(FC * f, FC * (f + 1))
+        gi = (dot(gs, WD[:, cols]) * dge[:, cols].astype(F32)).astype(BF)
+        VS[8:9, cols] = total(gi.astype(F32))
+        GD[:, cols] = dot(gst, hid[:, cols]).astype(BF)
+        GU[:, cols] = dot(lowt, gi).astype(BF)
+        acc2[...] += dot(gi, WU[:, cols], NT)
+    gf = acc2[...]
+    VS[3:4, :768] = total(gf * normed1)
+    VS[4:5, :768] = total(gf)
+    gsf = norm_back(gf * gain1, normed1, inv1)
+    GF[...] = gsf
+    gb = gsf.astype(BF)
+    VS[2:3, :768] = total(gb.astype(F32))
+    GC[...] = dot(gb, WO[...]).astype(BF)
+    GO[...] = dot(gsf.T.astype(BF), ctx).astype(BF)
+
+
+def feed_call(X, CT, WO, WU, WD, VEC, COT):
+    return pl.pallas_call(
+        feed_kernel,
+        out_shape=[sds((512, 768)), sds((512, 768), F32), sds((512, 768)), sds((768, 768)), sds((768, 3072)), sds((768, 3072)), sds((16, 3072), F32)],
+        in_specs=[VM] * 7,
+        out_specs=[VM] * 7,
+        scratch_shapes=[pltpu.VMEM((512, 3072), BF), pltpu.VMEM((512, 3072), BF), pltpu.VMEM((512, 768), F32), pltpu.VMEM((512, 768), F32)],
+        name="feed",
+        compiler_params=pltpu.CompilerParams(vmem_limit_bytes=60 * 2**20),
+    )(X, CT, WO, WU, WD, VEC, COT)
+
+
+def attend_back_kernel(E, Q, KT, V, CT, RS, GC, DQT, DK, DV, ebuf, gct, rcol, esem):
+    gct[...] = GC[...].astype(F32).T.astype(BF)
+    rcol[...] = RS[...].T
+    for i in range(2):
+        pltpu.make_async_copy(E.at[i], ebuf.at[i], esem.at[i]).start()
+
+    def pair(p, carry):
+        lanes = pl.ds(pl.multiple_of(128 * p, 128), 128)
+        vp = V[:, lanes]
+        qp = Q[:, lanes]
+        gp = GC[:, lanes].astype(F32)
+        half = lax.broadcasted_iota(jnp.int32, (512, 128), 1) // 64
+        dk = dv = None
+        for i in range(2):
+            h = 2 * p + i
+            rows = pl.ds(pl.multiple_of(64 * h, 64), 64)
+            rc = rcol[...]
+            sel = lax.broadcasted_iota(jnp.int32, rc.shape, 1) == h
+            r = jnp.sum(jnp.where(sel, rc, 0.0), axis=1, keepdims=True)
+            gm = jnp.where(half == i, gp * r, 0.0).astype(BF)
+            qm = jnp.where(half == i, qp, jnp.zeros_like(qp))
+            delta = jnp.sum(CT[rows, :].astype(F32) * gct[rows, :].astype(F32), axis=0, keepdims=True) * RS[pl.ds(h, 1), :]
+            pltpu.make_async_copy(E.at[h], ebuf.at[i], esem.at[i]).wait()
+            e = ebuf[i]
+            ds = (e.astype(F32) * (dot(vp, gm, NT) - delta)).astype(BF)
+            dvi = dot(e, gm)
+            dki = dot(ds, qm)
+            dv = dvi if i == 0 else dv + dvi
+            dk = dki if i == 0 else dk + dki
+            DQT[rows, :] = (dot(KT[rows, :], ds) * 0.125).astype(BF)
+
+            @pl.when(p < 5)
+            def _():
+                pltpu.make_async_copy(E.at[h + 2], ebuf.at[i], esem.at[i]).start()
+
+        DK[:, lanes] = dk.astype(BF)
+        DV[:, lanes] = dv.astype(BF)
+        return carry
+
+    lax.fori_loop(0, 6, pair, 0)
+
+
+def attend_back_call(E, Q, KT, V, CT, RS, GC):
+    return pl.pallas_call(
+        attend_back_kernel,
+        out_shape=[sds((768, 512)), sds((1024, 768)), sds((1024, 768))],
+        in_specs=[ANY] + [VM] * 6,
+        out_specs=[VM] * 3,
+        scratch_shapes=[pltpu.VMEM((2, 1024, 512), BF), pltpu.VMEM((768, 512), BF), pltpu.VMEM((512, 16), F32), pltpu.SemaphoreType.DMA((2,))],
+        name="attend_back",
+        compiler_params=pltpu.CompilerParams(vmem_limit_bytes=56 * 2**20),
+    )(E, Q, KT, V, CT, RS, GC)
+
+
+ROFF = (1, 3, 4, 5, 6)
+SUMS = []
+for _i in range(4):
+    SUMS += [("u", _i, XY), ("d", _i, YX)]
+SUMS += [("t", 3, XY), ("t", 0, YX), ("t", 1, XY), ("t", 2, YX)]
+GRADS_AT = 3
+
+
+def scatter_kernel(
+    X, DQT, DK, DV, GF, WT, GO, GU, GD, VS, OUT,
+    LO, IG, D4, DU, DD, VO,
+    gt, gu, gd, rt, ru, rd, dkr, dvr, igb, vpack, vrecv, vsum, vrecv2, pairs, pairr,
+    lsem, ks, kr, os_, or_, gs, gr, cs, cr, vs_, vr, ws, wr, ps, pr,
+):
+    y, c, z, x = place()
+    j = 2 * z + x
+    at = coords()
+    partner = device(y, 1 - c, z, x)
+    G, R = (gt, gu, gd), (rt, ru, rd)
+    loads = [
+        pltpu.make_async_copy(GU, gu, lsem.at[0]),
+        pltpu.make_async_copy(GD, gd, lsem.at[1]),
+        pltpu.make_async_copy(GO, gt.at[3], lsem.at[2]),
+    ]
+    for cp in loads:
+        cp.start()
+    greet_all()
+    sends = []
+
+    def remote(src, dst, send, recv, to, cond=True):
+        cp = pltpu.make_async_remote_copy(src_ref=src, dst_ref=dst, send_sem=send, recv_sem=recv, device_id=to, device_id_type=MESH)
+        if cond is True:
+            cp.start()
+        else:
+            pl.when(cond)(cp.start)
+        sends.append((cond, cp))
+        return cp
+
+    def arrive(dst, recv):
+        pltpu.make_async_remote_copy(src_ref=dst, dst_ref=dst, send_sem=recv, recv_sem=recv, device_id=partner, device_id_type=MESH).wait_recv()
+
+    theirs = pl.ds(pl.multiple_of(512 * (1 - c), 128), 512)
+    ours = pl.ds(pl.multiple_of(512 * c, 128), 512)
+    remote(DK.at[theirs], dkr, ks.at[0], kr.at[0], partner)
+    remote(DV.at[theirs], dvr, ks.at[1], kr.at[1], partner)
+
+    def tokens(src, dst, k, send, recv, loc):
+        b = 4 * c + k
+        mine = (x == c) & (b // 2 == z) & (b % 2 == x)
+        cp = pltpu.make_async_remote_copy(src_ref=src, dst_ref=dst, send_sem=send, recv_sem=recv, device_id=device(y, x, b // 2, b % 2), device_id_type=MESH)
+        lc = pltpu.make_async_copy(src, dst, loc)
+        pl.when(jnp.logical_not(mine))(cp.start)
+        pl.when(mine)(lc.start)
+        return mine, cp, lc
+
+    conds = []
+    for k in range(4):
+        conds.append(tokens(OUT.at[pl.ds(128 * k, 128)], LO.at[z], k, os_.at[0, k], or_.at[0, z], lsem.at[3]))
+
+    n = len(SUMS)
+
+    def slot(order, s):
+        def place_of(at):
+            spot = dict(at)
+            for d in order[s + 1 :]:
+                spot[d] = 1 - at[d]
+            return whole(spot, order[:s])
+        return place_of
+
+    def launch(u, s):
+        ch = SUMS[u]
+        order = ch[2]
+        to = flip(at, order[s])
+        src = region(G, ch, whole(to, order[:s]))
+        dst = region(R, ch, slot(order, s)(to))
+        for k in range(len(src)):
+            remote(src[k], dst[k], gs.at[u, s, k], gr.at[u, s, k], to_device(to))
+
+    def absorb(u, s):
+        ch = SUMS[u]
+        kind, i, order = ch
+        got = region(R, ch, slot(order, s)(at))
+        own = region(G, ch, whole(at, order[:s]))
+        for k in range(len(got)):
+            arrive(got[k], gr.at[u, s, k])
+            if s > 0:
+                own[k][...] = own[k][...] + got[k][...]
+                continue
+            done = own[k][...].astype(F32) + got[k][...].astype(F32)
+            if kind == "u":
+                DU[i] = done
+            elif kind == "d":
+                DD[i // 2, :, 384 * (i % 2) : 384 * (i % 2) + 384] = done
+            else:
+                lo, hi = done[:, :192], done[:, 192:]
+                D4[i, pl.ds(pl.multiple_of(48 * c, 16), 48), :] = jnp.where(c == 0, lo, hi)
+                pairs[i] = jnp.where(c == 0, hi, lo)
+                remote(pairs.at[i], pairr.at[i], ps.at[i], pr.at[i], partner)
+
+    def gradients():
+        arrive(dkr, kr.at[0])
+        arrive(dvr, kr.at[1])
+        dk = (DK[ours].astype(F32) + dkr[...].astype(F32)).astype(BF)
+        dv = (DV[ours].astype(F32) + dvr[...].astype(F32)).astype(BF)
+        xo = X[ours]
+        dqf = DQT[...].astype(F32).T
+        dq = dqf.astype(BF)
+        shape = (2, 2, 2, 2, 48, 768)
+        gt[0] = dot(DQT[...], xo).astype(BF).reshape(shape)
+        gt[1] = dot(dk.astype(F32).T.astype(BF), xo).astype(BF).reshape(shape)
+        gt[2] = dot(dv.astype(F32).T.astype(BF), xo).astype(BF).reshape(shape)
+        ig = GF[...] + dot(dq, WT[0]) + dot(dk, WT[1]) + dot(dv, WT[2])
+        igb[...] = ig.astype(BF)
+        for k in range(4):
+            conds.append(tokens(igb.at[pl.ds(128 * k, 128)], IG.at[z], k, os_.at[1, k], or_.at[1, z], lsem.at[4]))
+        qsum = jnp.sum(dqf, axis=0, keepdims=True)
+        vsm = jnp.sum(dv.astype(F32), axis=0, keepdims=True)
+        low = jnp.concatenate([qsum, vsm, VS[2:8, :768]], axis=0)
+        for b in range(8):
+            vpack[b] = jnp.zeros((16, 384), F32)
+            vpack[b, 0:8, 0:96] = low[:, 96 * b : 96 * b + 96]
+            vpack[b, 8:9, :] = VS[8:9, 384 * b : 384 * b + 384]
+        for d in range(1, 8):
+            o = (j + d) % 8
+            remote(vpack.at[o], vrecv.at[d], vs_.at[d], vr.at[d], device(y, c, o // 2, o % 2))
+
+    for t in range(n + ROFF[4]):
+        if t == 0:
+            loads[0].wait()
+        if t == 1:
+            loads[1].wait()
+        if t == 8:
+            loads[2].wait()
+        if t < n:
+            launch(t, 4)
+        if t == GRADS_AT:
+            gradients()
+        for s in range(5):
+            u = t - ROFF[s]
+            if 0 <= u < n:
+                absorb(u, 4 - s)
+                if s < 4:
+                    launch(u, 3 - s)
+        if t == GRADS_AT + 2:
+            total = vpack[j]
+            for d in range(1, 8):
+                arrive(vrecv.at[d], vr.at[d])
+                total = total + vrecv[d]
+            vsum[...] = total
+            me = 2 * y + c
+            for d in range(1, 4):
+                o = (me + d) % 4
+                remote(vsum, vrecv2.at[d], ws.at[d], wr.at[d], (o, j))
+        if t == GRADS_AT + 4:
+            total = vsum[...]
+            for d in range(1, 4):
+                arrive(vrecv2.at[d], wr.at[d])
+                total = total + vrecv2[d]
+            VO[...] = total
+    for i in range(4):
+        arrive(pairr.at[i], pr.at[i])
+        D4[i, pl.ds(pl.multiple_of(48 * (1 - c), 16), 48), :] = pairr[i]
+    for w, home in ((0, LO), (1, IG)):
+        for m in range(4):
+            mine = (m == z) & (x == c) & (z // 2 == c)
+
+            @pl.when(jnp.logical_not(mine))
+            def _(w=w, home=home, m=m):
+                arrive(home.at[m], or_.at[w, m])
+
+            @pl.when(mine)
+            def _(w=w, home=home, m=m):
+                pltpu.make_async_copy(home.at[m], home.at[m], lsem.at[3 + w]).wait()
+    for cond, cp in sends:
+        if cond is True:
+            cp.wait_send()
+        else:
+            pl.when(cond)(cp.wait_send)
+    for mine, cp, lc in conds:
+        pl.when(jnp.logical_not(mine))(cp.wait_send)
+
+
+def scatter_call(X, DQT, DK, DV, GF, WT, GO, GU, GD, VS, OUT):
+    S = pltpu.SemaphoreType.DMA
+    n = len(SUMS)
+    sets = [pltpu.VMEM((4, 2, 2, 2, 2, 48, 768), BF), pltpu.VMEM((2, 2, 4, 48, 3072), BF), pltpu.VMEM((2, 2, 2, 2, 48, 3072), BF)]
+    return pl.pallas_call(
+        scatter_kernel,
+        out_shape=[sds((4, 128, 768)), sds((4, 128, 768)), sds((4, 96, 192), F32), sds((4, 48, 384), F32), sds((2, 48, 768), F32), sds((16, 384), F32)],
+        in_specs=[VM, VM, VM, VM, VM, VM, ANY, ANY, ANY, VM, VM],
+        out_specs=[ANY, ANY, VM, VM, VM, VM],
+        scratch_shapes=sets + sets + [
+            pltpu.VMEM((512, 768), BF), pltpu.VMEM((512, 768), BF), pltpu.VMEM((512, 768), BF),
+            pltpu.VMEM((8, 16, 384), F32), pltpu.VMEM((8, 16, 384), F32), pltpu.VMEM((16, 384), F32), pltpu.VMEM((4, 16, 384), F32),
+            pltpu.VMEM((4, 48, 192), F32), pltpu.VMEM((4, 48, 192), F32),
+            S((5,)), S((2,)), S((2,)), S((2, 4)), S((2, 4)), S((n, 5, 4)), S((n, 5, 4)), S((4,)), S((4,)), S((8,)), S((8,)), S((4,)), S((4,)), S((4,)), S((4,)),
+        ],
+        name="scatter",
+        compiler_params=pltpu.CompilerParams(collective_id=2, has_side_effects=True, vmem_limit_bytes=60 * 2**20),
+    )(X, DQT, DK, DV, GF, WT, GO.reshape(2, 2, 2, 2, 48, 768), GU.reshape(2, 2, 4, 48, 3072), GD.reshape(2, 2, 2, 2, 48, 3072), VS, OUT)
+
+
+def rows_on_chips(*a):
+    xs,cot,seg,w4,wup,wdt,vec=prepare(a)
+    X,C,SEG,WT,WU,WD,VEC=gather_call(xs,cot,seg,w4,wup,wdt,vec)
+    X=X.reshape(1024,768); C=C.reshape(512,768); W=WT.reshape(4,768,768); WU=WU.reshape(768,3072); WD=WD.reshape(768,3072)
+    Q,KT,V,E,CT,RS=attend_call(X,W,SEG,VEC)
+    OUT,GF,GC,GO,GU,GD,VS=feed_call(X,CT,W[3],WU,WD,VEC,C)
+    DQT,DK,DV=attend_back_call(E,Q,KT,V,CT,RS,GC)
+    LO,IG,D4,DU,DD,VO=scatter_call(X,DQT,DK,DV,GF,W,GO,GU,GD,VS,OUT)
+    D4=D4.swapaxes(1,2)
+    DU=DU.reshape(192,384); DD=DD.reshape(96,768).T
+    v=VO[:8,:96]
+    s=(4,1,128,768)
+    return (LO.reshape(s),IG.reshape(s),D4[0],v[0],D4[1],D4[2],v[1],D4[3],v[2],v[3],v[4],DU,VO[8],DD,v[5],v[6],v[7])
 
 
 EPSILON = 1e-12
@@ -201,7 +897,7 @@
     )
 
 
-def on_device(
+def general(
     inputs,
     segment_ids,
     query_weight,
@@ -224,33 +920,33 @@
     outputs = []
     input_grads = []
     totals = None
+    widened = (
+        lax.all_gather(query_weight, "blk", axis=1, tiled=True),
+        lax.all_gather(key_weight, "blk", axis=1, tiled=True),
+        lax.all_gather(value_weight, "blk", axis=1, tiled=True),
+        lax.all_gather(output_weight, "blk", axis=1, tiled=True),
+        lax.all_gather(up_weight, "blk", axis=1, tiled=True),
+        lax.all_gather(down_weight, "blk", axis=1, tiled=True),
+        lax.all_gather(query_bias.reshape(1, -1), "blk", axis=1, tiled=True),
+        lax.all_gather(value_bias.reshape(1, -1), "blk", axis=1, tiled=True),
+        lax.all_gather(output_bias.reshape(1, -1), "blk", axis=1, tiled=True),
+        lax.all_gather(first_gain.reshape(1, -1), "blk", axis=1, tiled=True),
+        lax.all_gather(first_shift.reshape(1, -1), "blk", axis=1, tiled=True),
+        lax.all_gather(up_bias.reshape(1, -1), "blk", axis=1, tiled=True),
+        lax.all_gather(down_bias.reshape(1, -1), "blk", axis=1, tiled=True),
+        lax.all_gather(second_gain.reshape(1, -1), "blk", axis=1, tiled=True),
+        lax.all_gather(second_shift.reshape(1, -1), "blk", axis=1, tiled=True),
+    )
+    complete = (
+        lax.all_gather(widened[0], "dp", axis=0, tiled=True),
+        lax.all_gather(widened[1], "dp", axis=0, tiled=True),
+        lax.all_gather(widened[2], "dp", axis=0, tiled=True),
+        lax.all_gather(widened[3], "dp", axis=0, tiled=True),
+        lax.all_gather(widened[4], "dp", axis=0, tiled=True),
+        lax.all_gather(widened[5], "dp", axis=0, tiled=True),
+    )
+    shared = tuple(complete) + tuple(widened[6:])
     for batch_index in range(inputs.shape[0]):
-        widened = (
-            lax.all_gather(query_weight, "blk", axis=1, tiled=True),
-            lax.all_gather(key_weight, "blk", axis=1, tiled=True),
-            lax.all_gather(value_weight, "blk", axis=1, tiled=True),
-            lax.all_gather(output_weight, "blk", axis=1, tiled=True),
-            lax.all_gather(up_weight, "blk", axis=1, tiled=True),
-            lax.all_gather(down_weight, "blk", axis=1, tiled=True),
-            lax.all_gather(query_bias.reshape(1, -1), "blk", axis=1, tiled=True),
-            lax.all_gather(value_bias.reshape(1, -1), "blk", axis=1, tiled=True),
-            lax.all_gather(output_bias.reshape(1, -1), "blk", axis=1, tiled=True),
-            lax.all_gather(first_gain.reshape(1, -1), "blk", axis=1, tiled=True),
-            lax.all_gather(first_shift.reshape(1, -1), "blk", axis=1, tiled=True),
-            lax.all_gather(up_bias.reshape(1, -1), "blk", axis=1, tiled=True),
-            lax.all_gather(down_bias.reshape(1, -1), "blk", axis=1, tiled=True),
-            lax.all_gather(second_gain.reshape(1, -1), "blk", axis=1, tiled=True),
-            lax.all_gather(second_shift.reshape(1, -1), "blk", axis=1, tiled=True),
-        )
-        complete = (
-            lax.all_gather(widened[0], "dp", axis=0, tiled=True),
-            lax.all_gather(widened[1], "dp", axis=0, tiled=True),
-            lax.all_gather(widened[2], "dp", axis=0, tiled=True),
-            lax.all_gather(widened[3], "dp", axis=0, tiled=True),
-            lax.all_gather(widened[4], "dp", axis=0, tiled=True),
-            lax.all_gather(widened[5], "dp", axis=0, tiled=True),
-        )
-        shared = tuple(complete) + tuple(widened[6:])
         layer_out, layer_grad, contributions = micro_step(
             shared, inputs[batch_index], segment_ids[batch_index], cotangent[batch_index]
         )
@@ -360,6 +1056,13 @@
         P("blk"),
         P("blk"),
     )
+    small = mesh.shape["dp"] == 4 and mesh.shape["blk"] == 8
+
+    def on_device(*arrays):
+        if small and arrays[0].shape == (4, 1, 128, 768):
+            return rows_on_chips(*arrays)
+        return general(*arrays)
+
     return jax.shard_map(
         on_device, mesh=mesh, in_specs=in_specs, out_specs=out_specs, check_vma=False
     )

time: 2430 us -> 310 us (0.13)
  waiting for transfers between devices: 1460 us -> 0 us
  blocking collectives: 482 us -> 0 us
  matrix products: 294 us -> 0 us
  Pallas kernels: 0 us -> 283 us
  local copies, waits for them, and re-layouts: 116 us -> 25.8 us
  other arithmetic: 43.9 us -> 0.12 us
    unnamed x58 -> x0, waiting for transfers between devices: 645 us -> none
    reduce_scatter x8 -> x0, waiting for transfers between devices: 494 us -> none  [the longest x1 165 us: on_device(): lax.psum_scatter(totals[4], 'blk', scatter_dimension=1, tiled=True)]
    all_gather x21 -> x0, blocking collectives: 444 us -> none  [the longest x4 105 us: micro_step(): total_piece = lax.all_gather(sent[2], 'blk', axis=1, tiled=True)]
    all_gather x24 -> x0, waiting for transfers between devices: 319 us -> none  [the longest x4 113 us: micro_step(): key_piece = lax.all_gather(key_rows, 'blk', axis=1, tiled=True)]
    dot_general x96 -> x0, matrix products: 294 us -> none  [product(): return jnp.einsum(form, left, right, preferred_element_type=jnp.float32)]
    pallas_call x0 -> x5, Pallas kernels: none -> 283 us  [the longest x1 107 us: gather_call(): pl.pallas_call(gather_kernel, out_shape=[jax.ShapeDtypeStruct((8, 128, 76...]
    convert_element_type x28 -> x0, local copies, waits for them, and re-layouts: 46 us -> none  [the longest x4 10.7 us: micro_step(): context_piece.astype(jnp.bfloat16).reshape(row_count, count, HEADS, HD)]
    unnamed x1 -> x0, blocking collectives: 29.9 us -> none
  transfers between devices with their start and end apart: 45 -> 0, of which waited for: 30 -> 0; matrix products, arithmetic and copies ran while one was open for 18% -> 0% of each run, Pallas kernels for 0% -> 0%
where the time goes in v1:
time: 310 us
  Pallas kernels  283 us (91%)
  local copies, waits for them, and re-layouts  25.8 us (8%)
    pallas_call x1, Pallas kernels, gather_call(): pl.pallas_call(gather_kernel, out_shape=[jax.ShapeDtypeStruct((8, 128, 76...  107 us
    pallas_call x1, Pallas kernels, scatter_call(): pl.pallas_call(scatter_kernel, out_shape=[sds((4, 128, 768)), sds((4, 128...  106 us
    pallas_call x1, Pallas kernels, feed_call(): pl.pallas_call(feed_kernel, out_shape=[sds((512, 768)), sds((512, 768), F...  27.3 us
    pallas_call x1, Pallas kernels, attend_call(): pl.pallas_call(attend_kernel, out_shape=[sds((512, 768)), sds((768, 1024)...  22.8 us
    pallas_call x1, Pallas kernels, attend_back_call(): pl.pallas_call(attend_back_kernel, out_shape=[sds((768, 512)), sds((1024,...  20.1 us
    unnamed x38, local copies, waits for them, and re-layouts  17.8 us

profile of v1, /device:TPU:1, one launch (start us, length us, event | category | flops | bytes accessed | tf_op | source)
XLA Modules:
  0.0 309.7 jit_solution(9505807007505464300)
XLA Ops:
  0.7 0.1 pad.7.clone
  0.7 0.7 broadcast_in_dim.6
  1.4 0.8 stack.55
  2.2 0.1 fusion.2.vec
  2.3 0.9 copy.35
  3.2 0.9 copy.36
  4.1 0.9 copy.37
  5.0 0.9 copy.38
  5.9 0.0 copy-start.1
  5.9 1.1 copy-done.1
  7.1 0.0 copy-start.2
  7.1 1.1 copy-done.2
  8.2 0.0 copy-start.5
  8.2 0.9 copy-done.5
  9.1 0.0 copy-start.6
  9.1 0.9 copy-done.6
  10.0 0.0 copy-start.8
  10.0 0.7 copy-done.8
  10.7 107.3 %gather.1 = (bf16[8,128,768]{2,1,0:T(8,128)(2,1)S(1)}, bf16[4,128,768]{2,1,0:T(8,128)(2,1)S(1)}, s32[8,1,128]{2,1,0:T(1,128)S(1)}, bf16[4,2,2,2,2,48,768]{6,5,4,...) custom-call(bf16[4,128,768]{2,1,0:T(8,128)(2,1)S(1)} %bitcast.67, ...), custom_call_target="tpu_custom_call" | custom-call | tf_op jit(solution)/shard_map/gather/pallas_call | solution.py:241
  118.0 0.0 copy-start
  118.0 1.2 copy-done
  119.2 0.0 copy-start.3
  119.2 0.9 copy-done.3
  120.1 0.0 copy-start.4
  120.1 0.6 copy-done.4
  120.7 0.0 copy-start.7
  120.7 0.6 copy-done.7
  121.3 2.4 slice.52
  123.7 22.8 %attend.1 = (bf16[512,768]{1,0:T(8,128)(2,1)}, bf16[768,1024]{1,0:T(8,128)(2,1)}, bf16[1024,768]{1,0:T(8,128)(2,1)}, bf16[12,1024,512]{2,1,0:T(8,128)(2,1)}, bf1...) custom-call(bf16[1024,768]{1,0:T(8,128)(2,1)} %bitcast.64, bf16[4,768,768]{2,1,0:T(8,128)(2,1)} %bitcast.72, ...), custom_call_target="tpu_custom_call" | custom-call | tf_op jit(solution)/shard_map/attend/pallas_call | solution.py:344
  146.5 27.3 %feed.1 = (bf16[512,768]{1,0:T(8,128)(2,1)}, f32[512,768]{1,0:T(8,128)}, bf16[512,768]{1,0:T(8,128)(2,1)}, bf16[768,768]{1,0:T(8,128)(2,1)}, bf16[768,3072]{1,0:...) custom-call(bf16[1024,768]{1,0:T(8,128)(2,1)} %bitcast.65, bf16[768,512]{1,0:T(8,128)(2,1)} %get-tuple-element.54.CT, ...), custom_call_target="tpu_custom_call" | custom-call | tf_op jit(solution)/shard_map/feed/pallas_call | solution.py:426
  173.8 20.1 %attend_back.1 = (bf16[768,512]{1,0:T(8,128)(2,1)}, bf16[1024,768]{1,0:T(8,128)(2,1)}, bf16[1024,768]{1,0:T(8,128)(2,1)}) custom-call(bf16[12,1024,512]{2,1,0:T(8,128)(2,1)} %get-tuple-element.50.E, bf16[512,768]{1,0:T(8,128)(2,1)} %get-tuple-element.51.Q, bf16[768,1024]{1,0:T(8,128)(2,1)} %get-tuple-element.52.KT, bf16[1024,768]{1,0:T(8,128)(2,1)} %get-tuple-element.53.V, ...), custom_call_target="tpu_custom_call" | custom-call | tf_op jit(solution)/shard_map/attend_back/pallas_call | solution.py:480
  193.9 105.6 %scatter.1 = (bf16[4,128,768]{2,1,0:T(8,128)(2,1)}, bf16[4,128,768]{2,1,0:T(8,128)(2,1)}, f32[4,96,192]{2,1,0:T(8,128)}, f32[4,48,384]{2,1,0:T(8,128)}, f32[2,48,768]{2,1,0:T(8,128)}, /*index=5*/f32[16,384]{1,0:T(8,128)}) custom-call(bf16[1024,768]{1,0:T(8,128)(2,1)} %bitcast.66, bf16[768,512]{1,0:T(8,128)(2,1)} %get-tuple-element.60.DQT, ...), custom_call_target="tpu_custom_call" | custom-call | tf_op jit(solution)/shard_map/scatter/pallas_call | solution.py:677
  299.5 0.0 copy-start.10
  299.5 1.4 slice_reduce_fusion
  300.9 1.5 slice_bitcast_fusion.4
  302.4 0.0 copy-start.9
  302.4 1.1 slice_bitcast_fusion
  303.6 0.7 copy.44
  304.3 0.7 copy.43
  305.0 0.7 copy.42
  305.8 0.7 copy.41
  306.5 0.0 copy-done.10
  306.5 0.0 copy-start.12
  306.5 0.0 copy-start.11
  306.5 0.9 copy.49
  307.4 0.0 copy-done.9
  307.4 0.9 copy.50
  308.3 0.0 copy-done.12
  308.3 0.7 copy.51
  309.0 0.0 copy-done.11
  309.0 0.7 copy.52
  (2 shorter events, 0.0 us)
Async XLA Ops:
  5.9 1.1 copy-start.1
  7.1 1.1 copy-start.2
  8.2 0.9 copy-start.5
  9.1 0.9 copy-start.6
  10.0 0.7 copy-start.8
  118.0 1.2 copy-start
  119.2 0.9 copy-start.3
  120.1 0.6 copy-start.4
  120.7 0.6 copy-start.7
  299.5 7.0 %copy-start.10 = (bf16[4,128,768]{2,1,0:T(8,128)(2,1)S(1)}, bf16[4,128,768]{2,1,0:T(8,128)(2,1)}, u32[]{:S(2)}) copy-start(bf16[4,128,768]{2,1,0:T(8,128)(2,1)} %get-tuple-element.69) | copy-start | bytes 2359300
  302.4 5.0 %copy-start.9 = (bf16[4,128,768]{2,1,0:T(8,128)(2,1)S(1)}, bf16[4,128,768]{2,1,0:T(8,128)(2,1)}, u32[]{:S(2)}) copy-start(bf16[4,128,768]{2,1,0:T(8,128)(2,1)} %get-tuple-element.70) | copy-start | bytes 2359300
  306.5 1.8 copy-start.12
  306.5 2.5 copy-start.11
